TPU v7x, 256 devices: a whole 4x4x8 slice. The times are simulated.
256 devices in a mesh: expert: 64 (over y, z, core), tensor: 4 (over x).
Axes of the slice: x: 4, y: 4, z: 8, core: 2. Of those that a mesh axis runs over, the one named last changes fastest.
Arguments:
- tokens: bfloat16 [8192, 2048], P('expert', 'tensor'), may hold values from -6 to 6
- routes: int32 [8192, 6], P('expert'), may hold values from 0 to 63, all different within a row; in each aligned block of 128 rows (0 to 127, 128 to 255, ...) at most 24 rows name the same one
- route_weights: float32 [8192, 6], P('expert'), may hold values from 0.1 to 1
- w_gate: bfloat16 [64, 2048, 1408], P('expert', None, 'tensor'), may hold values from -0.125 to 0.125
- w_up: bfloat16 [64, 2048, 1408], P('expert', None, 'tensor'), may hold values from -0.125 to 0.125
- w_down: bfloat16 [64, 1408, 2048], P('expert', 'tensor'), may hold values from -0.15625 to 0.15625
Outputs:
- expert_mix: bfloat16 [8192, 2048], P('expert', 'tensor')
Inputs may be any that keep to these rules, and one draw needn't show every extreme that they name: `routes`: each token names 6 different experts; among the 128 tokens of one index of expert (aligned blocks of rows) no expert is named more than 24 times, and in some block some expert exactly 24 times.
All inputs are finite; a program needn't handle non-finite values.
Results may differ from a plain program's by a relative error of at most 0.018.
Values may be sent and summed in bfloat16 or wider, within the bound.
No kernel may reach another device: no remote copies, remote signals or barrier semaphores. Data moves between devices by JAX's collectives and lax.ppermute only.
A program may use at most 64 MiB of HBM per device.

v0:
```python
import jax
import jax.numpy as jnp
from jax import lax
from jax.sharding import PartitionSpec as P


def shards(tokens, routes, route_weights, w_gate, w_up, w_down):
    tok_rows, quarter = tokens.shape
    top_count = routes.shape[1]
    local_experts = w_gate.shape[0]
    groups = lax.axis_size("expert")
    experts = local_experts * groups
    capacity = min(tok_rows, 2 * tok_rows * top_count // experts)
    slots_total = experts * capacity
    flat_routes = routes.reshape(-1)
    onehot = (flat_routes[:, None] == jnp.arange(experts, dtype=jnp.int32)[None, :]).astype(
        jnp.int32
    )
    slot_rank = jnp.sum((jnp.cumsum(onehot, axis=0) - 1) * onehot, axis=1)
    slot_index = flat_routes * capacity + slot_rank
    placed = slot_index[:, None] == jnp.arange(slots_total, dtype=jnp.int32)[None, :]
    placed = placed.reshape(tok_rows, top_count, slots_total)
    pick_matrix = jnp.sum(placed.astype(jnp.float32), axis=1).astype(jnp.bfloat16)
    outgoing = lax.dot_general(
        pick_matrix, tokens, (((0,), (0,)), ((), ())), preferred_element_type=jnp.float32
    )
    outgoing = outgoing.astype(jnp.bfloat16).reshape(groups, local_experts * capacity, quarter)
    incoming = lax.all_to_all(outgoing, "expert", split_axis=0, concat_axis=0, tiled=True)
    incoming = incoming.reshape(groups, local_experts, capacity, quarter)
    slot_rows = incoming[:, 0]
    flat_rows = slot_rows.reshape(groups * capacity, quarter)
    gate_w = w_gate[0]
    up_w = w_up[0]
    shard_piece = lax.all_gather(flat_rows, "tensor", axis=1, tiled=True)
    gate_sum = jnp.dot(shard_piece, gate_w, preferred_element_type=jnp.float32)
    up_sum = jnp.dot(shard_piece, up_w, preferred_element_type=jnp.float32)
    hidden = (jax.nn.silu(gate_sum) * up_sum).astype(jnp.bfloat16)
    partial_value = jnp.dot(hidden, w_down[0], preferred_element_type=jnp.float32)
    summed = lax.psum_scatter(
        partial_value.astype(jnp.bfloat16), "tensor", scatter_dimension=1, tiled=True
    )
    results = [summed.reshape(groups, capacity, quarter)]
    returning = jnp.stack(results, axis=1).reshape(groups, local_experts * capacity, quarter)
    returned = lax.all_to_all(returning, "expert", split_axis=0, concat_axis=0, tiled=True)
    returned = returned.reshape(slots_total, quarter)
    picked = jnp.take(returned, slot_index, axis=0).reshape(tok_rows, top_count, quarter)
    expert_mix = jnp.sum(route_weights[:, :, None] * picked.astype(jnp.float32), axis=1)
    return expert_mix.astype(jnp.bfloat16)


def solution(mesh):
    placed = (
        P("expert", "tensor"),
        P("expert", None),
        P("expert", None),
        P("expert", None, "tensor"),
        P("expert", None, "tensor"),
        P("expert", "tensor", None),
    )
    return jax.shard_map(
        shards, mesh=mesh, in_specs=placed, out_specs=P("expert", "tensor"), check_vma=False
    )
```

profile of v0, /device:TPU:32, one launch (start us, length us, event | category | flops | bytes accessed | tf_op | source)
XLA Modules:
  0.0 278.4 jit_solution(17561297441441996238)
XLA Ops:
  6.5 0.0 all-gather.2.cloned.1.call-start
  6.5 0.9 copy.22
  7.4 0.1 eq.40
  7.6 0.1 reshape.85
  7.7 1.8 reduce-window.6
  9.5 0.3 slice_reduce_fusion
  9.8 0.1 fusion.9
  10.0 0.1 reduce_sum.32
  10.1 0.1 copy.25
  10.2 0.7 compare_and_fusion
  10.9 0.7 convert_reduce_fusion
  11.6 1.5 convolution_convert_fusion.1
  13.1 0.0 copy-start.3
  13.1 50.9 %all_to_all.10 = bf16[64,24,512]{2,1,0:T(8,128)(2,1)} all-to-all(bf16[64,24,512]{2,1,0:T(8,128)(2,1)S(1)} %bitcast.37), channel_id=1, replica_groups=mesh['expert'=64,'tensor'=4] {'expert'}, dimensions={0} | all-to-all | bytes 3145728 | tf_op jit(solution)/shard_map/all_to_all | solution.py:28
  64.0 0.0 all-gather.2.cloned.1.call-update
  64.1 0.0 reduce-scatter.2.cloned.1.call-start
  64.1 66.0 %all-gather.2.cloned.1.call-done = bf16[1536,2048]{1,0:T(8,128)(2,1)} async-done(((bf16[1536,512]{1,0:T(8,128)(2,1)}), bf16[1536,2048]{1,0:T(8,128)(2,1)}) %all-gather.2.cloned.1.call-update) | async-done | bytes 6291472 | tf_op jit(solution)/shard_map/all_gather | solution.py:34
  130.1 6.6 %fusion.3 = f32[1536,352]{0,1:T(8,128)} fusion(bf16[1536,2048]{1,0:T(8,128)(2,1)} %all-gather.2.cloned.1.call-done, bf16[1,2048,352]{1,2,0:T(8,128)(2,1)S(1)} %copy-done.3), kind=kOutput, calls=%fused_computation.10 | convolution fusion | flops 2214592512 | bytes 9895936 | tf_op jit(solution)/shard_map/dot_general | solution.py:35
  136.6 11.8 %convolution_convert_fusion = bf16[1536,2048]{1,0:T(8,128)(2,1)} fusion(bf16[1,352,2048]{2,1,0:T(8,128)(2,1)S(1)} %copy-done, bf16[1536,2048]{1,0:T(8,128)(2,1)} %all-gather.2.cloned.1.call-done, f32[1536,352]{0,1:T(8,128)} %fusion.3, bf16[1,2048,352]{1,2,0:T(8,128)(2,1)} %param.10), kind=kOutput, calls=%fused_computation.1 | convolution fusion | flops 4435574784 | bytes 17629184 | tf_op jit(solution)/shard_map/dot_general | solution.py:38
  148.4 0.0 reduce-scatter.2.cloned.1.call-update
  148.4 0.0 copy-start.1
  148.5 0.0 copy-start.2
  148.5 67.3 %reduce-scatter.2.cloned.1.call-done = bf16[1536,512]{1,0:T(8,128)(2,1)} async-done(((bf16[1536,2048]{1,0:T(8,128)(2,1)}), bf16[1536,512]{1,0:T(8,128)(2,1)}) %reduce-scatter.2.cloned.1.call-update) | async-done | bytes 1572880 | tf_op jit(solution)/shard_map/reduce_scatter | solution.py:39
  215.8 10.5 %all-to-all-start.1 = ((bf16[64,24,512]{2,1,0:T(8,128)(2,1)}), bf16[64,24,512]{2,1,0:T(8,128)(2,1)S(1)}, u32[]{:S(2)}, u32[]{:S(2)}) async-start(bf16[64,24,512]{2,1,0:T(8,128)(2,1)} %bitcast.38), calls=%async_computation.2 | async-start | bytes 3145728 | tf_op jit(solution)/shard_map/all_to_all | solution.py:44
  226.3 0.1 copy.27
  226.4 0.1 mul.46
  226.6 0.1 copy.26
  226.7 0.1 copy.21
  226.9 38.5 %all-to-all-done.1 = bf16[64,24,512]{2,1,0:T(8,128)(2,1)S(1)} async-done(((bf16[64,24,512]{2,1,0:T(8,128)(2,1)}), bf16[64,24,512]{2,1,0:T(8,128)(2,1)S(1)}, u32[]{:S(2)}, u32[]{:S(2)}) %all-to-all-start.1) | async-done | bytes 1572896 | tf_op jit(solution)/shard_map/all_to_all | solution.py:44
  265.4 3.3 %gather_fusion = bf16[768,512]{1,0:T(8,128)(2,1)} fusion(bf16[1536,512]{1,0:T(8,128)(2,1)S(1)} %bitcast.35, s32[1024]{0:T(1024)S(1)} %pad_clamp_fusion), kind=kCustom, calls=%fused_computation | custom fusion | bytes 1575936 | tf_op jit(solution)/shard_map/jit(_take)/gather | solution.py:46
  268.7 1.3 gather.7
  270.0 1.5 multiply_reduce_fusion
  (10 shorter events, 0.1 us)
Async XLA Ops:
  6.5 130.1 %copy-start = (bf16[1,352,2048]{2,1,0:T(8,128)(2,1)S(1)}, bf16[1,352,2048]{2,1,0:T(8,128)(2,1)}, u32[]{:S(2)}) copy-start(bf16[1,352,2048]{2,1,0:T(8,128)(2,1)} %param.11) | copy-start | bytes 4325380
  6.5 123.5 %all-gather.2.cloned.1.call-start = ((), (), s32[]{:S(2)}) async-start(), calls=%async_computation.3 | async-start | bytes 7864320 | tf_op jit(solution)/shard_map/all_gather | solution.py:34
  13.1 116.9 %copy-start.3 = (bf16[1,2048,352]{1,2,0:T(8,128)(2,1)S(1)}, bf16[1,2048,352]{1,2,0:T(8,128)(2,1)}, u32[]{:S(2)}) copy-start(bf16[1,2048,352]{1,2,0:T(8,128)(2,1)} %param.9) | copy-start | bytes 4325380
  64.1 151.8 %reduce-scatter.2.cloned.1.call-start = ((), (), s32[]{:S(2)}) async-start(), calls=%async_computation.4 | async-start | bytes 7864320 | tf_op jit(solution)/shard_map/reduce_scatter | solution.py:39
  148.4 77.9 %copy-start.1 = (s32[128,6]{0,1:T(8,128)S(1)}, s32[128,6]{0,1:T(8,128)}, u32[]{:S(2)}) copy-start(s32[128,6]{0,1:T(8,128)} %param.7) | copy-start | bytes 9220
  148.5 78.3 %copy-start.2 = (f32[128,6]{0,1:T(8,128)S(1)}, f32[128,6]{0,1:T(8,128)}, u32[]{:S(2)}) copy-start(f32[128,6]{0,1:T(8,128)} %param.8) | copy-start | bytes 9220
  215.8 49.6 %all-to-all-start.1 = ((bf16[64,24,512]{2,1,0:T(8,128)(2,1)}), bf16[64,24,512]{2,1,0:T(8,128)(2,1)S(1)}, u32[]{:S(2)}, u32[]{:S(2)}) async-start(bf16[64,24,512]{2,1,0:T(8,128)(2,1)} %bitcast.38), calls=%async_computation.2 | async-start | bytes 3145728 | tf_op jit(solution)/shard_map/all_to_all | solution.py:44
Sparse Core Ops, SparseCore 0:
  64.2 65.8 all-gather.1
  148.6 67.1 reduce-scatter.1
where the time goes:
time: 281 us; the launch traced here: 278 us
  waiting for transfers between devices  172 us (61%)
  blocking collectives  50.9 us (18%)
  matrix products  19.9 us (7%)
  between operations  13.5 us (5%)
  starting transfers between devices  10.5 us (4%)
  local copies, waits for them, and re-layouts  6.8 us (2%)
  other arithmetic  4.94 us (2%)
    reduce_scatter x1, waiting for transfers between devices, shards(): lax.psum_scatter(partial_value.astype(jnp.bfloat16), 'tensor', scatter_di...  67.3 us
    all_gather x1, waiting for transfers between devices, shards(): shard_piece = lax.all_gather(flat_rows, 'tensor', axis=1, tiled=True)  66 us
    all_to_all x1, blocking collectives, shards(): lax.all_to_all(outgoing, 'expert', split_axis=0, concat_axis=0, tiled=True)  50.9 us
    all_to_all x1, waiting for transfers between devices, shards(): lax.all_to_all(returning, 'expert', split_axis=0, concat_axis=0, tiled=True)  38.5 us
    dot_general x1, matrix products, shards(): jnp.dot(hidden, w_down[0], preferred_element_type=jnp.float32)  11.8 us
    all_to_all x1, starting transfers between devices, shards(): lax.all_to_all(returning, 'expert', split_axis=0, concat_axis=0, tiled=True)  10.5 us
    dot_general x1, matrix products, shards(): gate_sum = jnp.dot(shard_piece, gate_w, preferred_element_type=jnp.float32)  6.58 us
  transfers between devices with their start and end apart: 3, of which 3 were waited for; matrix products, arithmetic and copies ran while one was open for 0% of the time, Pallas kernels for 0%

commit v1 on v0

v1 whole, which is shorter than its diff:
```python
import functools

import jax
import jax.numpy as jnp
import numpy as np
from jax import lax
from jax.experimental import pallas as pl
from jax.experimental.pallas import tpu as pltpu
from jax.sharding import Mesh
from jax.sharding import PartitionSpec as P

CAP = 24
SLOTS = 8
VMEM = pl.BlockSpec(memory_space=pltpu.VMEM)
SMEM = pl.BlockSpec(memory_space=pltpu.SMEM)
LIMIT = 20 * 1024 * 1024


def call(kernel, outs, flops=0, moved=0):
    scalars = [SMEM]

    def run(*args):
        return pl.pallas_call(
            kernel,
            out_shape=outs,
            in_specs=scalars + [VMEM] * (len(args) - 1),
            out_specs=jax.tree.map(lambda _: VMEM, outs),
            compiler_params=pltpu.CompilerParams(vmem_limit_bytes=LIMIT),
            cost_estimate=pl.CostEstimate(flops=flops, bytes_accessed=moved, transcendentals=0),
        )(*args)

    return run


def ranked(x_ref, routes_ref, lanes, step, weights_ref=None):
    tokens = routes_ref.shape[1]
    swap = x_ref[0] // 2
    rows = lax.broadcasted_iota(jnp.int32, (lanes, tokens), 0)
    named, slot = (rows // SLOTS) * step, rows % SLOTS
    routes = routes_ref[...] ^ swap
    member = jnp.zeros((lanes, tokens), jnp.float32)
    weight = jnp.zeros((lanes, tokens), jnp.float32)
    for k in range(routes.shape[0]):
        hit = routes[k : k + 1, :] == named
        member = jnp.where(hit, 1.0, member)
        if weights_ref is not None:
            weight = jnp.where(hit, weights_ref[k : k + 1, :], weight)
    earlier = lax.broadcasted_iota(jnp.int32, (tokens, tokens), 0)
    later = lax.broadcasted_iota(jnp.int32, (tokens, tokens), 1)
    before = jnp.where(earlier < later, 1.0, 0.0).astype(jnp.bfloat16)
    rank = jnp.dot(member.astype(jnp.bfloat16), before, preferred_element_type=jnp.float32)
    return jnp.where(member > 0.0, rank, -1.0), slot, weight


def pick_kernel(x_ref, routes_ref, tokens_ref, *outs):
    rank, slot, _ = ranked(x_ref, routes_ref, outs[0].shape[0], 1)
    tokens = tokens_ref[...]
    for chunk, out in enumerate(outs):
        pick = jnp.where(rank == (slot + chunk * SLOTS).astype(jnp.float32), 1.0, 0.0).astype(jnp.bfloat16)
        out[...] = jnp.dot(pick, tokens, preferred_element_type=jnp.float32).astype(jnp.bfloat16)


def weigh_kernel(x_ref, routes_ref, weights_ref, *outs):
    rank, slot, weight = ranked(x_ref, routes_ref, outs[0].shape[0], 2, weights_ref)
    for chunk, out in enumerate(outs):
        out[...] = jnp.where(rank == (slot + chunk * SLOTS).astype(jnp.float32), weight, 0.0)


def columns_kernel(x_ref, down_ref, mine_ref, theirs_ref):
    x = x_ref[0]
    quarter = mine_ref.shape[1] // 2

    def part(q):
        return down_ref[:, pl.ds(pl.multiple_of(q * quarter, quarter), quarter)]

    mine_ref[:, :quarter] = part(x)
    mine_ref[:, quarter:] = part(x ^ 3)
    theirs_ref[:, :quarter] = part(x ^ 1)
    theirs_ref[:, quarter:] = part(x ^ 2)


def along(value, weight):
    return lax.dot_general(value, weight, (((1,), (1,)), ((), ())), preferred_element_type=jnp.float32)


def hidden_kernel(x_ref, own, near, far, across, gate0, up0, gate1, up1, out):
    x = x_ref[0]
    quarter = own.shape[1]
    pieces = [(own, x), (near, x ^ 1), (far, x ^ 3), (across, x ^ 2)]
    for half, (gate_ref, up_ref) in enumerate(((gate0, up0), (gate1, up1))):
        gate, up = 0.0, 0.0
        for ref, q in pieces:
            span = pl.ds(pl.multiple_of(q * quarter, quarter), quarter)
            value = ref[...]
            gate = gate + along(value, gate_ref[:, span])
            up = up + along(value, up_ref[:, span])
        out[half] = (gate / (1.0 + jnp.exp(-gate)) * up).astype(jnp.bfloat16)


def down_kernel(x_ref, here, there, down0, down1, down2, down3, out):
    total = jnp.dot(here[0], down0[...], preferred_element_type=jnp.float32)
    total = total + jnp.dot(here[1], down1[...], preferred_element_type=jnp.float32)
    total = total + jnp.dot(there[0], down2[...], preferred_element_type=jnp.float32)
    total = total + jnp.dot(there[1], down3[...], preferred_element_type=jnp.float32)
    out[...] = total.astype(jnp.bfloat16)


def across_rows(weight, value):
    return lax.dot_general(weight, value, (((0,), (0,)), ((), ())), preferred_element_type=jnp.float32)


def mixed(weight, value):
    high = weight.astype(jnp.bfloat16)
    low = (weight - high.astype(jnp.float32)).astype(jnp.bfloat16)
    return across_rows(high, value) + across_rows(low, value)


def mix_first_kernel(x_ref, weight, value, out):
    out[...] = mixed(weight[...], value[...])


def mix_kernel(x_ref, total, weight, value, out):
    out[...] = total[...] + mixed(weight[...], value[...])


def mix_last_kernel(x_ref, total, weight, value, keep, send):
    half = keep.shape[1]
    done = total[...] + mixed(weight[...], value[...])
    keep[...] = done[:, :half]
    send[...] = done[:, half:].astype(jnp.bfloat16)


def move_x(value, flip):
    return lax.ppermute(value, "x", [(i, i ^ flip) for i in range(4)])


def move_core(value):
    return lax.ppermute(value, "c", [(0, 1), (1, 0)])


def to_group(value):
    pairs = []
    for x in range(4):
        for core in range(2):
            stays = (x // 2) == core
            target = (x, 1 - core) if stays else (x ^ 3, core)
            pairs.append((core * 4 + x, target[1] * 4 + target[0]))
    return lax.ppermute(value, ("c", "x"), pairs)


def shards(tokens, routes, route_weights, w_gate, w_up, w_down):
    rows, quarter = tokens.shape
    half_ff = w_gate.shape[2]
    routes, route_weights = routes.T, route_weights.T
    w_gate, w_up = jnp.swapaxes(w_gate, 1, 2), jnp.swapaxes(w_up, 1, 2)
    chips = 32
    chunks = CAP // SLOTS
    at = chips * SLOTS
    me = lax.axis_index("x").astype(jnp.int32).reshape(1)
    bf16, f32 = jnp.bfloat16, jnp.float32

    def shape(*dims, dtype=bf16):
        return jax.ShapeDtypeStruct(dims, dtype)

    outgoing = call(pick_kernel, [shape(2 * at, quarter)] * chunks)(me, routes, tokens)
    mixing = call(weigh_kernel, [shape(at, rows, dtype=f32)] * chunks)(me, routes, route_weights)

    gate0, up0 = to_group(w_gate[0]), to_group(w_up[0])
    gate1, up1 = move_core(gate0), move_core(up0)
    own_down = to_group(w_down[0])
    down0, theirs = call(columns_kernel, [shape(half_ff, 2 * quarter)] * 2)(me, own_down)
    down1 = move_core(down0)
    down2 = move_x(theirs, 1)
    down3 = move_core(down2)

    total = None
    for chunk in range(chunks):
        sent = outgoing[chunk].reshape(chips, 2 * SLOTS, quarter)
        incoming = lax.all_to_all(sent, ("y", "z"), split_axis=0, concat_axis=0, tiled=True)
        own = incoming[:, :SLOTS].reshape(at, quarter)
        other = incoming[:, SLOTS:].reshape(at, quarter)
        near, far, across = move_x(own, 1), move_x(other, 3), move_x(other, 2)
        hidden = call(hidden_kernel, shape(2, at, half_ff), flops=2 * at * 4 * quarter * 4 * half_ff)(
            me, own, near, far, across, gate0, up0, gate1, up1
        )
        beside = move_x(hidden, 1)
        result = call(down_kernel, shape(at, 2 * quarter), flops=2 * at * 4 * half_ff * 2 * quarter)(
            me, hidden, beside, down0, down1, down2, down3
        )
        result = result.reshape(chips, SLOTS, 2 * quarter)
        returned = lax.all_to_all(result, ("y", "z"), split_axis=0, concat_axis=0, tiled=True)
        returned = returned.reshape(at, 2 * quarter)
        if chunk == 0:
            total = call(mix_first_kernel, shape(rows, 2 * quarter, dtype=f32))(me, mixing[0], returned)
        elif chunk < chunks - 1:
            total = call(mix_kernel, shape(rows, 2 * quarter, dtype=f32))(me, total, mixing[chunk], returned)
        else:
            keep, send = call(mix_last_kernel, [shape(rows, quarter, dtype=f32), shape(rows, quarter)])(
                me, total, mixing[chunk], returned
            )
    return (keep + move_x(send, 3).astype(f32)).astype(bf16)


def solution(mesh):
    fine = Mesh(mesh.devices.reshape(4, 8, 2, 4), ("y", "z", "c", "x"))
    expert = ("y", "z", "c")
    placed = (
        P(expert, "x"),
        P(expert, None),
        P(expert, None),
        P(expert, None, "x"),
        P(expert, None, "x"),
        P(expert, "x", None),
    )
    return jax.shard_map(shards, mesh=fine, in_specs=placed, out_specs=P(expert, "x"), check_vma=False)
```

time: 281 us -> 223 us (0.79)
  starting transfers between devices: 10.5 us -> 82.4 us
  waiting for transfers between devices: 172 us -> 102 us
  blocking collectives: 50.9 us -> 0 us
  Pallas kernels: 0 us -> 28.1 us
  matrix products: 19.9 us -> 0 us
  between operations: 13.5 us -> 0.2 us
  other arithmetic: 4.94 us -> 0.68 us
    ppermute x0 -> x21, waiting for transfers between devices: none -> 71.5 us  [the longest x14 61.6 us: move_x(): return lax.ppermute(value, 'x', [(i, i ^ flip) for i in range(4)])]
    reduce_scatter x1 -> x0, waiting for transfers between devices: 67.3 us -> none  [shards(): lax.psum_scatter(partial_value.astype(jnp.bfloat16), 'tensor', scatter_di...]
    all_gather x1 -> x0, waiting for transfers between devices: 66 us -> none  [shards(): shard_piece = lax.all_gather(flat_rows, 'tensor', axis=1, tiled=True)]
    all_to_all x1 -> x0, blocking collectives: 50.9 us -> none  [shards(): lax.all_to_all(outgoing, 'expert', split_axis=0, concat_axis=0, tiled=True)]
    all_to_all x1 -> x6, starting transfers between devices: 10.5 us -> 58.5 us  [the longest x3 30.8 us: shards(): lax.all_to_all(result, ('y', 'z'), split_axis=0, concat_axis=0, tiled=True)]
    pallas_call x0 -> x12, Pallas kernels: none -> 28.1 us  [run(): pl.pallas_call(kernel, out_shape=outs, in_specs=scalars + [VMEM] * (len(a...]
    ppermute x0 -> x21, starting transfers between devices: none -> 23.9 us  [the longest x14 20.3 us: move_x(): return lax.ppermute(value, 'x', [(i, i ^ flip) for i in range(4)])]
    dot_general x3 -> x0, matrix products: 19.9 us -> none  [the longest x1 11.8 us: shards(): jnp.dot(hidden, w_down[0], preferred_element_type=jnp.float32)]
  transfers between devices with their start and end apart: 3 -> 27, of which waited for: 3 -> 15; matrix products, arithmetic and copies ran while one was open for 0% -> 2% of each run, Pallas kernels for 0% -> 13%
where the time goes in v1:
time: 223 us; the launch traced here: 222 us
  waiting for transfers between devices  102 us (46%)
  starting transfers between devices  82.4 us (37%)
  Pallas kernels  28.1 us (13%)
  local copies, waits for them, and re-layouts  9 us (4%)
    ppermute x14, waiting for transfers between devices, move_x(): return lax.ppermute(value, 'x', [(i, i ^ flip) for i in range(4)])  61.6 us
    all_to_all x3, starting transfers between devices, shards(): lax.all_to_all(result, ('y', 'z'), split_axis=0, concat_axis=0, tiled=True)  30.8 us
    pallas_call x12, Pallas kernels, run(): pl.pallas_call(kernel, out_shape=outs, in_specs=scalars + [VMEM] * (len(a...  28.1 us
    all_to_all x3, starting transfers between devices, shards(): lax.all_to_all(sent, ('y', 'z'), split_axis=0, concat_axis=0, tiled=True)  27.7 us
    ppermute x14, starting transfers between devices, move_x(): return lax.ppermute(value, 'x', [(i, i ^ flip) for i in range(4)])  20.3 us
    all_to_all x3, waiting for transfers between devices, shards(): lax.all_to_all(sent, ('y', 'z'), split_axis=0, concat_axis=0, tiled=True)  18.3 us
    all_to_all x3, waiting for transfers between devices, shards(): lax.all_to_all(result, ('y', 'z'), split_axis=0, concat_axis=0, tiled=True)  11.8 us
    ppermute x3, waiting for transfers between devices, to_group(): return lax.ppermute(value, ('c', 'x'), pairs)  9.86 us
  transfers between devices with their start and end apart: 27, of which 15 were waited for; matrix products, arithmetic and copies ran while one was open for 2% of the time, Pallas kernels for 13%

profile of v1, /device:TPU:32, one launch (start us, length us, event | category | flops | bytes accessed | tf_op | source)
XLA Modules:
  0.0 222.0 jit_solution(15956505036988508211)
XLA Ops:
  0.0 2.3 %collective-permute-start.4 = (bf16[352,2048]{1,0:T(8,128)(2,1)}, bf16[352,2048]{1,0:T(8,128)(2,1)S(1)}, u32[]{:S(2)}, u32[]{:S(2)}) collective-permute-start(bf16[352,2048]{1,0:T(8,128)(2,1)} %bitcast.38), channel_id=1, source_target_pairs={{0,4},{4,7},{1,5},{5,6},{2,1},{6,2},{3,0},{7,3},{8,12},{12,15},{9,... | collective-permute-start | bytes 4325384 | tf_op jit(solution)/shard_map/ppermute | solution.py:148
  6.2 11.4 %all-to-all-start.2 = ((bf16[32,16,512]{2,1,0:T(8,128)(2,1)}), bf16[32,16,512]{2,1,0:T(8,128)(2,1)S(1)}, u32[]{:S(2)}, u32[]{:S(2)}) async-start(bf16[32,16,512]{2,1,0:T(8,128)(2,1)} %bitcast.13), calls=%async_computation.2 | async-start | bytes 1048576 | tf_op jit(solution)/shard_map/all_to_all | solution.py:179
  17.8 18.3 %all-to-all-done.2 = bf16[32,16,512]{2,1,0:T(8,128)(2,1)S(1)} async-done(((bf16[32,16,512]{2,1,0:T(8,128)(2,1)}), bf16[32,16,512]{2,1,0:T(8,128)(2,1)S(1)}, u32[]{:S(2)}, u32[]{:S(2)}) %all-to-all-start.2) | async-done | bytes 524320 | tf_op jit(solution)/shard_map/all_to_all | solution.py:179
  36.1 4.9 %all-to-all-start.4 = ((bf16[32,16,512]{2,1,0:T(8,128)(2,1)}), bf16[32,16,512]{2,1,0:T(8,128)(2,1)}, u32[]{:S(2)}, u32[]{:S(2)}) async-start(bf16[32,16,512]{2,1,0:T(8,128)(2,1)} %bitcast.18), calls=%async_computation.4 | async-start | bytes 1048576 | tf_op jit(solution)/shard_map/all_to_all | solution.py:179
  41.6 9.9 %collective-permute-done.8.down_ref = bf16[352,2048]{1,0:T(8,128)(2,1)} collective-permute-done((bf16[352,2048]{1,0:T(8,128)(2,1)}, bf16[352,2048]{1,0:T(8,128)(2,1)}, u32[]{:S(2)}, u32[]{:S(2)}) %collective-permute-start.8) | collective-permute-done | bytes 1441824 | tf_op jit(solution)/shard_map/ppermute | solution.py:148
  51.4 2.4 %shard_map.67 = (bf16[352,1024]{1,0:T(8,128)(2,1)S(1)}, bf16[352,1024]{1,0:T(8,128)(2,1)}) custom-call(s32[1]{0:T(128)} %bitcast.x_ref, bf16[352,2048]{1,0:T(8,128)(2,1)} %collective-permute-done.8.down_ref), custom_call_target="tpu_custom_call" | custom-call | tf_op jit(solution)/shard_map/pallas_call | solution.py:23
  55.0 1.8 slice_bitcast_fusion.2
  58.5 11.4 %all-to-all-start = ((bf16[32,16,512]{2,1,0:T(8,128)(2,1)}), bf16[32,16,512]{2,1,0:T(8,128)(2,1)}, u32[]{:S(2)}, u32[]{:S(2)}) async-start(bf16[32,16,512]{2,1,0:T(8,128)(2,1)} %bitcast.33), calls=%async_computation | async-start | bytes 1048576 | tf_op jit(solution)/shard_map/all_to_all | solution.py:179
  69.9 6.7 %collective-permute-done.12.near = bf16[256,512]{1,0:T(8,128)(2,1)S(1)} collective-permute-done((bf16[256,512]{1,0:T(8,128)(2,1)S(1)}, bf16[256,512]{1,0:T(8,128)(2,1)S(1)}, u32[]{:S(2)}, u32[]{:S(2)}) %collective-permute-start.12) | collective-permute-done | bytes 262176 | tf_op jit(solution)/shard_map/ppermute | solution.py:134
  76.6 2.2 collective-permute-start.14
  79.4 6.8 %collective-permute-done.14.across = bf16[256,512]{1,0:T(8,128)(2,1)S(1)} collective-permute-done((bf16[256,512]{1,0:T(8,128)(2,1)}, bf16[256,512]{1,0:T(8,128)(2,1)S(1)}, u32[]{:S(2)}, u32[]{:S(2)}) %collective-permute-start.14) | collective-permute-done | bytes 262176 | tf_op jit(solution)/shard_map/ppermute | solution.py:134
  86.3 4.2 %shard_map.70.here = bf16[2,256,352]{2,1,0:T(8,128)(2,1)S(1)} custom-call(s32[1]{0:T(128)} %bitcast.x_ref, bf16[256,512]{1,0:T(8,128)(2,1)S(1)} %get-tuple-element.28.own, bf16[256,512]{1,0:T(8,128)(2,1)S(1)} %collective-permute-done.12.near, bf16[256,512]{1,0:T(8,128)(2,1)} %collective-permute-done.13.far, ...), custom_call_target="tpu_custom_call" | custom-call | flops 1476395008 | tf_op jit(solution)/shard_map/pallas_call | solution.py:23
  91.3 9.8 %collective-permute-done.15.there = bf16[2,256,352]{2,1,0:T(8,128)(2,1)S(1)} collective-permute-done((bf16[2,256,352]{2,1,0:T(8,128)(2,1)S(1)}, bf16[2,256,352]{2,1,0:T(8,128)(2,1)S(1)}, u32[]{:S(2)}, u32[]{:S(2)}) %collective-permute-start.15) | collective-permute-done | bytes 360480 | tf_op jit(solution)/shard_map/ppermute | solution.py:134
  101.1 3.2 %shard_map.71 = bf16[256,1024]{1,0:T(8,128)(2,1)} custom-call(s32[1]{0:T(128)} %bitcast.x_ref, bf16[2,256,352]{2,1,0:T(8,128)(2,1)S(1)} %shard_map.70.here, bf16[2,256,352]{2,1,0:T(8,128)(2,1)S(1)} %collective-permute-done.15.there, bf16[352,1024]{1,0:T(8,128)(2,1)S(1)} %copy-done.1, bf16[352,1024]{1,0:T(8,128)(2,1)S(1)} %collective-permute-done.9.down1, ...), custom_call_target="tpu_custom_call" | custom-call | flops 738197504 | tf_op jit(solution)/shard_map/pallas_call | solution.py:23
  106.1 11.2 %all-to-all-start.3 = ((bf16[32,8,1024]{2,1,0:T(8,128)(2,1)}), bf16[32,8,1024]{2,1,0:T(8,128)(2,1)S(1)}, u32[]{:S(2)}, u32[]{:S(2)}) async-start(bf16[32,8,1024]{2,1,0:T(8,128)(2,1)} %bitcast.16), calls=%async_computation.3 | async-start | bytes 1048576 | tf_op jit(solution)/shard_map/all_to_all | solution.py:191
  119.1 3.7 %collective-permute-start.1 = (bf16[256,512]{1,0:T(8,128)(2,1)S(1)}, bf16[256,512]{1,0:T(8,128)(2,1)S(1)}, u32[]{:S(2)}, u32[]{:S(2)}) collective-permute-start(bf16[256,512]{1,0:T(8,128)(2,1)S(1)} %get-tuple-element.29), channel_id=1, source_target_pairs={{0,3},{1,2},{2,1},{3,0},{4,7},{5,6},{6,5},{7,4},{8,11},{9,10},{10,... | collective-permute-start | bytes 786440 | tf_op jit(solution)/shard_map/ppermute | solution.py:134
  123.5 3.7 %collective-permute-done.near = bf16[256,512]{1,0:T(8,128)(2,1)S(1)} collective-permute-done((bf16[256,512]{1,0:T(8,128)(2,1)S(1)}, bf16[256,512]{1,0:T(8,128)(2,1)S(1)}, u32[]{:S(2)}, u32[]{:S(2)}) %collective-permute-start) | collective-permute-done | bytes 262176 | tf_op jit(solution)/shard_map/ppermute | solution.py:134
  127.2 5.1 %collective-permute-done.1.far = bf16[256,512]{1,0:T(8,128)(2,1)S(1)} collective-permute-done((bf16[256,512]{1,0:T(8,128)(2,1)S(1)}, bf16[256,512]{1,0:T(8,128)(2,1)S(1)}, u32[]{:S(2)}, u32[]{:S(2)}) %collective-permute-start.1) | collective-permute-done | bytes 262176 | tf_op jit(solution)/shard_map/ppermute | solution.py:134
  134.0 4.1 %shard_map.66.here = bf16[2,256,352]{2,1,0:T(8,128)(2,1)S(1)} custom-call(s32[1]{0:T(128)} %bitcast.x_ref, bf16[256,512]{1,0:T(8,128)(2,1)S(1)} %get-tuple-element.30.own, bf16[256,512]{1,0:T(8,128)(2,1)S(1)} %collective-permute-done.near, bf16[256,512]{1,0:T(8,128)(2,1)S(1)} %collective-permute-done.1.far, ...), custom_call_target="tpu_custom_call" | custom-call | flops 1476395008 | tf_op jit(solution)/shard_map/pallas_call | solution.py:23
  138.2 8.8 %collective-permute-done.7.there = bf16[2,256,352]{2,1,0:T(8,128)(2,1)S(1)} collective-permute-done((bf16[2,256,352]{2,1,0:T(8,128)(2,1)S(1)}, bf16[2,256,352]{2,1,0:T(8,128)(2,1)S(1)}, u32[]{:S(2)}, u32[]{:S(2)}) %collective-permute-start.7) | collective-permute-done | bytes 360480 | tf_op jit(solution)/shard_map/ppermute | solution.py:134
  147.0 3.1 %shard_map.68 = bf16[256,1024]{1,0:T(8,128)(2,1)} custom-call(s32[1]{0:T(128)} %bitcast.x_ref, bf16[2,256,352]{2,1,0:T(8,128)(2,1)S(1)} %shard_map.66.here, bf16[2,256,352]{2,1,0:T(8,128)(2,1)S(1)} %collective-permute-done.7.there, bf16[352,1024]{1,0:T(8,128)(2,1)S(1)} %copy-done.2, bf16[352,1024]{1,0:T(8,128)(2,1)S(1)} %copy-done.5, ...), custom_call_target="tpu_custom_call" | custom-call | flops 738197504 | tf_op jit(solution)/shard_map/pallas_call | solution.py:23
  150.2 9.8 %all-to-all-start.1 = ((bf16[32,8,1024]{2,1,0:T(8,128)(2,1)}), bf16[32,8,1024]{2,1,0:T(8,128)(2,1)}, u32[]{:S(2)}, u32[]{:S(2)}) async-start(bf16[32,8,1024]{2,1,0:T(8,128)(2,1)} %bitcast.11), calls=%async_computation.1 | async-start | bytes 1048576 | tf_op jit(solution)/shard_map/all_to_all | solution.py:191
  161.5 2.7 %collective-permute-start.17 = (bf16[256,512]{1,0:T(8,128)(2,1)S(1)}, bf16[256,512]{1,0:T(8,128)(2,1)S(1)}, u32[]{:S(2)}, u32[]{:S(2)}) collective-permute-start(bf16[256,512]{1,0:T(8,128)(2,1)S(1)} %get-tuple-element.25), channel_id=1, source_target_pairs={{0,3},{1,2},{2,1},{3,0},{4,7},{5,6},{6,5},{7,4},{8,11},{9,10},{10,... | collective-permute-start | bytes 786440 | tf_op jit(solution)/shard_map/ppermute | solution.py:134
  165.4 3.2 %collective-permute-done.16.near = bf16[256,512]{1,0:T(8,128)(2,1)S(1)} collective-permute-done((bf16[256,512]{1,0:T(8,128)(2,1)S(1)}, bf16[256,512]{1,0:T(8,128)(2,1)S(1)}, u32[]{:S(2)}, u32[]{:S(2)}) %collective-permute-start.16) | collective-permute-done | bytes 262176 | tf_op jit(solution)/shard_map/ppermute | solution.py:134
  168.5 3.7 %collective-permute-done.17.far = bf16[256,512]{1,0:T(8,128)(2,1)S(1)} collective-permute-done((bf16[256,512]{1,0:T(8,128)(2,1)S(1)}, bf16[256,512]{1,0:T(8,128)(2,1)S(1)}, u32[]{:S(2)}, u32[]{:S(2)}) %collective-permute-start.17) | collective-permute-done | bytes 262176 | tf_op jit(solution)/shard_map/ppermute | solution.py:134
  174.0 4.1 %shard_map.73.here = bf16[2,256,352]{2,1,0:T(8,128)(2,1)S(1)} custom-call(s32[1]{0:T(128)} %bitcast.x_ref, bf16[256,512]{1,0:T(8,128)(2,1)S(1)} %get-tuple-element.26.own, bf16[256,512]{1,0:T(8,128)(2,1)S(1)} %collective-permute-done.16.near, bf16[256,512]{1,0:T(8,128)(2,1)S(1)} %collective-permute-done.17.far, ...), custom_call_target="tpu_custom_call" | custom-call | flops 1476395008 | tf_op jit(solution)/shard_map/pallas_call | solution.py:23
  178.6 7.5 %collective-permute-done.19.there = bf16[2,256,352]{2,1,0:T(8,128)(2,1)S(1)} collective-permute-done((bf16[2,256,352]{2,1,0:T(8,128)(2,1)S(1)}, bf16[2,256,352]{2,1,0:T(8,128)(2,1)S(1)}, u32[]{:S(2)}, u32[]{:S(2)}) %collective-permute-start.19) | collective-permute-done | bytes 360480 | tf_op jit(solution)/shard_map/ppermute | solution.py:134
  186.1 3.1 %shard_map.74 = bf16[256,1024]{1,0:T(8,128)(2,1)} custom-call(s32[1]{0:T(128)} %bitcast.x_ref, bf16[2,256,352]{2,1,0:T(8,128)(2,1)S(1)} %shard_map.73.here, bf16[2,256,352]{2,1,0:T(8,128)(2,1)S(1)} %collective-permute-done.19.there, bf16[352,1024]{1,0:T(8,128)(2,1)S(1)} %copy-done.3, bf16[352,1024]{1,0:T(8,128)(2,1)S(1)} %copy-done.6, ...), custom_call_target="tpu_custom_call" | custom-call | flops 738197504 | tf_op jit(solution)/shard_map/pallas_call | solution.py:23
  189.2 9.8 %all-to-all-start.5 = ((bf16[32,8,1024]{2,1,0:T(8,128)(2,1)}), bf16[32,8,1024]{2,1,0:T(8,128)(2,1)S(1)}, u32[]{:S(2)}, u32[]{:S(2)}) async-start(bf16[32,8,1024]{2,1,0:T(8,128)(2,1)} %bitcast.21), calls=%async_computation.5 | async-start | bytes 1048576 | tf_op jit(solution)/shard_map/all_to_all | solution.py:191
  201.0 11.8 %all-to-all-done.5 = bf16[32,8,1024]{2,1,0:T(8,128)(2,1)S(1)} async-done(((bf16[32,8,1024]{2,1,0:T(8,128)(2,1)}), bf16[32,8,1024]{2,1,0:T(8,128)(2,1)S(1)}, u32[]{:S(2)}, u32[]{:S(2)}) %all-to-all-start.5) | async-done | bytes 524320 | tf_op jit(solution)/shard_map/all_to_all | solution.py:191
  213.1 5.2 %collective-permute-start.20 = (bf16[128,512]{1,0:T(8,128)(2,1)S(1)}, bf16[128,512]{1,0:T(8,128)(2,1)S(1)}, u32[]{:S(2)}, u32[]{:S(2)}) collective-permute-start(bf16[128,512]{1,0:T(8,128)(2,1)S(1)} %get-tuple-element.24), channel_id=1, source_target_pairs={{0,3},{1,2},{2,1},{3,0},{4,7},{5,6},{6,5},{7,4},{8,11},{9,10},{10,... | collective-permute-start | bytes 393224 | tf_op jit(solution)/shard_map/ppermute | solution.py:134
  218.4 2.9 %collective-permute-done.20 = bf16[128,512]{1,0:T(8,128)(2,1)S(1)} collective-permute-done((bf16[128,512]{1,0:T(8,128)(2,1)S(1)}, bf16[128,512]{1,0:T(8,128)(2,1)S(1)}, u32[]{:S(2)}, u32[]{:S(2)}) %collective-permute-start.20) | collective-permute-done | bytes 131104 | tf_op jit(solution)/shard_map/ppermute | solution.py:134
  (70 shorter events, 23.0 us)
Async XLA Ops:
  0.0 41.0 %collective-permute-start.3 = (bf16[352,2048]{1,0:T(8,128)(2,1)}, bf16[352,2048]{1,0:T(8,128)(2,1)S(1)}, u32[]{:S(2)}, u32[]{:S(2)}) collective-permute-start(bf16[352,2048]{1,0:T(8,128)(2,1)} %bitcast.37), channel_id=1, source_target_pairs={{0,4},{4,7},{1,5},{5,6},{2,1},{6,2},{3,0},{7,3},{8,12},{12,15},{9,... | collective-permute-start | bytes 4325384 | tf_op jit(solution)/shard_map/ppermute | solution.py:148
  0.0 41.1 %collective-permute-start.4 = (bf16[352,2048]{1,0:T(8,128)(2,1)}, bf16[352,2048]{1,0:T(8,128)(2,1)S(1)}, u32[]{:S(2)}, u32[]{:S(2)}) collective-permute-start(bf16[352,2048]{1,0:T(8,128)(2,1)} %bitcast.38), channel_id=1, source_target_pairs={{0,4},{4,7},{1,5},{5,6},{2,1},{6,2},{3,0},{7,3},{8,12},{12,15},{9,... | collective-permute-start | bytes 4325384 | tf_op jit(solution)/shard_map/ppermute | solution.py:148
  6.2 29.9 %all-to-all-start.2 = ((bf16[32,16,512]{2,1,0:T(8,128)(2,1)}), bf16[32,16,512]{2,1,0:T(8,128)(2,1)S(1)}, u32[]{:S(2)}, u32[]{:S(2)}) async-start(bf16[32,16,512]{2,1,0:T(8,128)(2,1)} %bitcast.13), calls=%async_computation.2 | async-start | bytes 1048576 | tf_op jit(solution)/shard_map/all_to_all | solution.py:179
  17.6 33.8 %collective-permute-start.8 = (bf16[352,2048]{1,0:T(8,128)(2,1)}, bf16[352,2048]{1,0:T(8,128)(2,1)}, u32[]{:S(2)}, u32[]{:S(2)}) collective-permute-start(bf16[352,2048]{1,0:T(8,128)(2,1)} %bitcast.39), channel_id=1, source_target_pairs={{0,4},{4,7},{1,5},{5,6},{2,1},{6,2},{3,0},{7,3},{8,12},{12,15},{9,... | collective-permute-start | bytes 4325384 | tf_op jit(solution)/shard_map/ppermute | solution.py:148
  36.1 22.4 %all-to-all-start.4 = ((bf16[32,16,512]{2,1,0:T(8,128)(2,1)}), bf16[32,16,512]{2,1,0:T(8,128)(2,1)}, u32[]{:S(2)}, u32[]{:S(2)}) async-start(bf16[32,16,512]{2,1,0:T(8,128)(2,1)} %bitcast.18), calls=%async_computation.4 | async-start | bytes 1048576 | tf_op jit(solution)/shard_map/all_to_all | solution.py:179
  41.0 45.3 %collective-permute-start.5 = (bf16[352,2048]{1,0:T(8,128)(2,1)S(1)}, bf16[352,2048]{1,0:T(8,128)(2,1)}, u32[]{:S(2)}, u32[]{:S(2)}) collective-permute-start(bf16[352,2048]{1,0:T(8,128)(2,1)S(1)} %collective-permute-done.3.gate0), channel_id=1, source_target_pairs={{0,4},{4,0},{1,5},{5,1},{2,6},{6,2},{3,7},{7,3},{8,12},{12,8},{9,1... | collective-permute-start | bytes 4325384 | tf_op jit(solution)/shard_map/ppermute | solution.py:138
  41.1 45.2 %collective-permute-start.6 = (bf16[352,2048]{1,0:T(8,128)(2,1)S(1)}, bf16[352,2048]{1,0:T(8,128)(2,1)}, u32[]{:S(2)}, u32[]{:S(2)}) collective-permute-start(bf16[352,2048]{1,0:T(8,128)(2,1)S(1)} %collective-permute-done.4.up0), channel_id=1, source_target_pairs={{0,4},{4,0},{1,5},{5,1},{2,6},{6,2},{3,7},{7,3},{8,12},{12,8},{9,1... | collective-permute-start | bytes 4325384 | tf_op jit(solution)/shard_map/ppermute | solution.py:138
  54.7 24.7 %collective-permute-start.10 = (bf16[352,1024]{1,0:T(8,128)(2,1)}, bf16[352,1024]{1,0:T(8,128)(2,1)}, u32[]{:S(2)}, u32[]{:S(2)}) collective-permute-start(bf16[352,1024]{1,0:T(8,128)(2,1)} %get-tuple-element.18), channel_id=1, source_target_pairs={{0,1},{1,0},{2,3},{3,2},{4,5},{5,4},{6,7},{7,6},{8,9},{9,8},{10,11... | collective-permute-start | bytes 2162696 | tf_op jit(solution)/shard_map/ppermute | solution.py:134
  56.8 19.8 %collective-permute-start.12 = (bf16[256,512]{1,0:T(8,128)(2,1)S(1)}, bf16[256,512]{1,0:T(8,128)(2,1)S(1)}, u32[]{:S(2)}, u32[]{:S(2)}) collective-permute-start(bf16[256,512]{1,0:T(8,128)(2,1)S(1)} %get-tuple-element.28.own), channel_id=1, source_target_pairs={{0,1},{1,0},{2,3},{3,2},{4,5},{5,4},{6,7},{7,6},{8,9},{9,8},{10,11... | collective-permute-start | bytes 786440 | tf_op jit(solution)/shard_map/ppermute | solution.py:134
  58.5 20.3 %collective-permute-start.13 = (bf16[256,512]{1,0:T(8,128)(2,1)}, bf16[256,512]{1,0:T(8,128)(2,1)}, u32[]{:S(2)}, u32[]{:S(2)}) collective-permute-start(bf16[256,512]{1,0:T(8,128)(2,1)} %get-tuple-element.27), channel_id=1, source_target_pairs={{0,3},{1,2},{2,1},{3,0},{4,7},{5,6},{6,5},{7,4},{8,11},{9,10},{10,... | collective-permute-start | bytes 786440 | tf_op jit(solution)/shard_map/ppermute | solution.py:134
  58.5 47.5 %all-to-all-start = ((bf16[32,16,512]{2,1,0:T(8,128)(2,1)}), bf16[32,16,512]{2,1,0:T(8,128)(2,1)}, u32[]{:S(2)}, u32[]{:S(2)}) async-start(bf16[32,16,512]{2,1,0:T(8,128)(2,1)} %bitcast.33), calls=%async_computation | async-start | bytes 1048576 | tf_op jit(solution)/shard_map/all_to_all | solution.py:179
  76.6 9.7 %collective-permute-start.14 = (bf16[256,512]{1,0:T(8,128)(2,1)}, bf16[256,512]{1,0:T(8,128)(2,1)S(1)}, u32[]{:S(2)}, u32[]{:S(2)}) collective-permute-start(bf16[256,512]{1,0:T(8,128)(2,1)} %get-tuple-element.27), channel_id=1, source_target_pairs={{0,2},{1,3},{2,0},{3,1},{4,6},{5,7},{6,4},{7,5},{8,10},{9,11},{10,... | collective-permute-start | bytes 786440 | tf_op jit(solution)/shard_map/ppermute | solution.py:134
  78.8 12.5 %collective-permute-start.9 = (bf16[352,1024]{1,0:T(8,128)(2,1)}, bf16[352,1024]{1,0:T(8,128)(2,1)S(1)}, u32[]{:S(2)}, u32[]{:S(2)}) collective-permute-start(bf16[352,1024]{1,0:T(8,128)(2,1)} %copy-done), channel_id=1, source_target_pairs={{0,4},{4,0},{1,5},{5,1},{2,6},{6,2},{3,7},{7,3},{8,12},{12,8},{9,1... | collective-permute-start | bytes 2162696 | tf_op jit(solution)/shard_map/ppermute | solution.py:138
  79.3 12.0 %collective-permute-start.11 = (bf16[352,1024]{1,0:T(8,128)(2,1)}, bf16[352,1024]{1,0:T(8,128)(2,1)S(1)}, u32[]{:S(2)}, u32[]{:S(2)}) collective-permute-start(bf16[352,1024]{1,0:T(8,128)(2,1)} %collective-permute-done.10.down2), channel_id=1, source_target_pairs={{0,4},{4,0},{1,5},{5,1},{2,6},{6,2},{3,7},{7,3},{8,12},{12,8},{9,1... | collective-permute-start | bytes 2162696 | tf_op jit(solution)/shard_map/ppermute | solution.py:138
  90.5 10.6 %collective-permute-start.15 = (bf16[2,256,352]{2,1,0:T(8,128)(2,1)S(1)}, bf16[2,256,352]{2,1,0:T(8,128)(2,1)S(1)}, u32[]{:S(2)}, u32[]{:S(2)}) collective-permute-start(bf16[2,256,352]{2,1,0:T(8,128)(2,1)S(1)} %shard_map.70.here), channel_id=1, source_target_pairs={{0,1},{1,0},{2,3},{3,2},{4,5},{5,4},{6,7},{7,6},{8,9},{9,8},{10,11... | collective-permute-start | bytes 1081352 | tf_op jit(solution)/shard_map/ppermute | solution.py:134
  106.1 44.1 %all-to-all-start.3 = ((bf16[32,8,1024]{2,1,0:T(8,128)(2,1)}), bf16[32,8,1024]{2,1,0:T(8,128)(2,1)S(1)}, u32[]{:S(2)}, u32[]{:S(2)}) async-start(bf16[32,8,1024]{2,1,0:T(8,128)(2,1)} %bitcast.16), calls=%async_computation.3 | async-start | bytes 1048576 | tf_op jit(solution)/shard_map/all_to_all | solution.py:191
  118.3 8.9 %collective-permute-start = (bf16[256,512]{1,0:T(8,128)(2,1)S(1)}, bf16[256,512]{1,0:T(8,128)(2,1)S(1)}, u32[]{:S(2)}, u32[]{:S(2)}) collective-permute-start(bf16[256,512]{1,0:T(8,128)(2,1)S(1)} %get-tuple-element.30.own), channel_id=1, source_target_pairs={{0,1},{1,0},{2,3},{3,2},{4,5},{5,4},{6,7},{7,6},{8,9},{9,8},{10,11... | collective-permute-start | bytes 786440 | tf_op jit(solution)/shard_map/ppermute | solution.py:134
  119.1 27.9 %copy-start.2 = (bf16[352,1024]{1,0:T(8,128)(2,1)S(1)}, bf16[352,1024]{1,0:T(8,128)(2,1)}, u32[]{:S(2)}) copy-start(bf16[352,1024]{1,0:T(8,128)(2,1)} %copy-done) | copy-start | bytes 2162692
  119.1 27.9 %copy-start.5 = (bf16[352,1024]{1,0:T(8,128)(2,1)S(1)}, bf16[352,1024]{1,0:T(8,128)(2,1)}, u32[]{:S(2)}) copy-start(bf16[352,1024]{1,0:T(8,128)(2,1)} %copy-done.4) | copy-start | bytes 2162692
  119.1 27.9 %copy-start.8 = (bf16[352,1024]{1,0:T(8,128)(2,1)S(1)}, bf16[352,1024]{1,0:T(8,128)(2,1)}, u32[]{:S(2)}) copy-start(bf16[352,1024]{1,0:T(8,128)(2,1)} %copy-done.7) | copy-start | bytes 2162692
  119.1 13.1 %collective-permute-start.1 = (bf16[256,512]{1,0:T(8,128)(2,1)S(1)}, bf16[256,512]{1,0:T(8,128)(2,1)S(1)}, u32[]{:S(2)}, u32[]{:S(2)}) collective-permute-start(bf16[256,512]{1,0:T(8,128)(2,1)S(1)} %get-tuple-element.29), channel_id=1, source_target_pairs={{0,3},{1,2},{2,1},{3,0},{4,7},{5,6},{6,5},{7,4},{8,11},{9,10},{10,... | collective-permute-start | bytes 786440 | tf_op jit(solution)/shard_map/ppermute | solution.py:134
  122.9 11.1 %collective-permute-start.2 = (bf16[256,512]{1,0:T(8,128)(2,1)S(1)}, bf16[256,512]{1,0:T(8,128)(2,1)S(1)}, u32[]{:S(2)}, u32[]{:S(2)}) collective-permute-start(bf16[256,512]{1,0:T(8,128)(2,1)S(1)} %get-tuple-element.29), channel_id=1, source_target_pairs={{0,2},{1,3},{2,0},{3,1},{4,6},{5,7},{6,4},{7,5},{8,10},{9,11},{10,... | collective-permute-start | bytes 786440 | tf_op jit(solution)/shard_map/ppermute | solution.py:134
  138.1 8.9 %collective-permute-start.7 = (bf16[2,256,352]{2,1,0:T(8,128)(2,1)S(1)}, bf16[2,256,352]{2,1,0:T(8,128)(2,1)S(1)}, u32[]{:S(2)}, u32[]{:S(2)}) collective-permute-start(bf16[2,256,352]{2,1,0:T(8,128)(2,1)S(1)} %shard_map.66.here), channel_id=1, source_target_pairs={{0,1},{1,0},{2,3},{3,2},{4,5},{5,4},{6,7},{7,6},{8,9},{9,8},{10,11... | collective-permute-start | bytes 1081352 | tf_op jit(solution)/shard_map/ppermute | solution.py:134
  150.2 39.1 %all-to-all-start.1 = ((bf16[32,8,1024]{2,1,0:T(8,128)(2,1)}), bf16[32,8,1024]{2,1,0:T(8,128)(2,1)}, u32[]{:S(2)}, u32[]{:S(2)}) async-start(bf16[32,8,1024]{2,1,0:T(8,128)(2,1)} %bitcast.11), calls=%async_computation.1 | async-start | bytes 1048576 | tf_op jit(solution)/shard_map/all_to_all | solution.py:191
  161.1 7.5 %collective-permute-start.16 = (bf16[256,512]{1,0:T(8,128)(2,1)S(1)}, bf16[256,512]{1,0:T(8,128)(2,1)S(1)}, u32[]{:S(2)}, u32[]{:S(2)}) collective-permute-start(bf16[256,512]{1,0:T(8,128)(2,1)S(1)} %get-tuple-element.26.own), channel_id=1, source_target_pairs={{0,1},{1,0},{2,3},{3,2},{4,5},{5,4},{6,7},{7,6},{8,9},{9,8},{10,11... | collective-permute-start | bytes 786440 | tf_op jit(solution)/shard_map/ppermute | solution.py:134
  161.5 24.6 %copy-start.6 = (bf16[352,1024]{1,0:T(8,128)(2,1)S(1)}, bf16[352,1024]{1,0:T(8,128)(2,1)}, u32[]{:S(2)}) copy-start(bf16[352,1024]{1,0:T(8,128)(2,1)} %copy-done.4) | copy-start | bytes 2162692
  161.5 24.6 %copy-start.9 = (bf16[352,1024]{1,0:T(8,128)(2,1)S(1)}, bf16[352,1024]{1,0:T(8,128)(2,1)}, u32[]{:S(2)}) copy-start(bf16[352,1024]{1,0:T(8,128)(2,1)} %copy-done.7) | copy-start | bytes 2162692
  161.5 10.8 %collective-permute-start.17 = (bf16[256,512]{1,0:T(8,128)(2,1)S(1)}, bf16[256,512]{1,0:T(8,128)(2,1)S(1)}, u32[]{:S(2)}, u32[]{:S(2)}) collective-permute-start(bf16[256,512]{1,0:T(8,128)(2,1)S(1)} %get-tuple-element.25), channel_id=1, source_target_pairs={{0,3},{1,2},{2,1},{3,0},{4,7},{5,6},{6,5},{7,4},{8,11},{9,10},{10,... | collective-permute-start | bytes 786440 | tf_op jit(solution)/shard_map/ppermute | solution.py:134
  164.1 9.9 %collective-permute-start.18 = (bf16[256,512]{1,0:T(8,128)(2,1)S(1)}, bf16[256,512]{1,0:T(8,128)(2,1)S(1)}, u32[]{:S(2)}, u32[]{:S(2)}) collective-permute-start(bf16[256,512]{1,0:T(8,128)(2,1)S(1)} %get-tuple-element.25), channel_id=1, source_target_pairs={{0,2},{1,3},{2,0},{3,1},{4,6},{5,7},{6,4},{7,5},{8,10},{9,11},{10,... | collective-permute-start | bytes 786440 | tf_op jit(solution)/shard_map/ppermute | solution.py:134
  178.2 7.9 %collective-permute-start.19 = (bf16[2,256,352]{2,1,0:T(8,128)(2,1)S(1)}, bf16[2,256,352]{2,1,0:T(8,128)(2,1)S(1)}, u32[]{:S(2)}, u32[]{:S(2)}) collective-permute-start(bf16[2,256,352]{2,1,0:T(8,128)(2,1)S(1)} %shard_map.73.here), channel_id=1, source_target_pairs={{0,1},{1,0},{2,3},{3,2},{4,5},{5,4},{6,7},{7,6},{8,9},{9,8},{10,11... | collective-permute-start | bytes 1081352 | tf_op jit(solution)/shard_map/ppermute | solution.py:134
  189.2 23.6 %all-to-all-start.5 = ((bf16[32,8,1024]{2,1,0:T(8,128)(2,1)}), bf16[32,8,1024]{2,1,0:T(8,128)(2,1)S(1)}, u32[]{:S(2)}, u32[]{:S(2)}) async-start(bf16[32,8,1024]{2,1,0:T(8,128)(2,1)} %bitcast.21), calls=%async_computation.5 | async-start | bytes 1048576 | tf_op jit(solution)/shard_map/all_to_all | solution.py:191
  213.1 8.2 %collective-permute-start.20 = (bf16[128,512]{1,0:T(8,128)(2,1)S(1)}, bf16[128,512]{1,0:T(8,128)(2,1)S(1)}, u32[]{:S(2)}, u32[]{:S(2)}) collective-permute-start(bf16[128,512]{1,0:T(8,128)(2,1)S(1)} %get-tuple-element.24), channel_id=1, source_target_pairs={{0,3},{1,2},{2,1},{3,0},{4,7},{5,6},{6,5},{7,4},{8,11},{9,10},{10,... | collective-permute-start | bytes 393224 | tf_op jit(solution)/shard_map/ppermute | solution.py:134
  (11 other events, 112.2 us)

commit v2 on v1

v2 whole, which is shorter than its diff:
```python
import functools

import jax
import jax.numpy as jnp
import numpy as np
from jax import lax
from jax.experimental import pallas as pl
from jax.experimental.pallas import tpu as pltpu
from jax.sharding import Mesh
from jax.sharding import PartitionSpec as P

SLOTS = 8
CAP = 24
VMEM = pl.BlockSpec(memory_space=pltpu.VMEM)
SMEM = pl.BlockSpec(memory_space=pltpu.SMEM)
LIMIT = 60 * 1024 * 1024


def call(kernel, outs, flops=0, moved=0):
    def run(*args):
        return pl.pallas_call(
            kernel,
            out_shape=outs,
            in_specs=[SMEM] + [VMEM] * (len(args) - 1),
            out_specs=jax.tree.map(lambda _: VMEM, outs),
            compiler_params=pltpu.CompilerParams(vmem_limit_bytes=16 * 1024 * 1024),
            cost_estimate=pl.CostEstimate(flops=flops, bytes_accessed=moved, transcendentals=0),
        )(*args)

    return run


def ranked(x_ref, routes_ref, slots, step, weights_ref=None):
    tokens = routes_ref.shape[1]
    lanes = 64 // step * slots
    swap = x_ref[0] // 2
    rows = lax.broadcasted_iota(jnp.int32, (lanes, tokens), 0)
    named, slot = (rows // slots) * step, rows % slots
    routes = routes_ref[...] ^ swap
    member = jnp.zeros((lanes, tokens), jnp.float32)
    weight = jnp.zeros((lanes, tokens), jnp.float32)
    for k in range(routes.shape[0]):
        hit = routes[k : k + 1, :] == named
        member = jnp.where(hit, 1.0, member)
        if weights_ref is not None:
            weight = jnp.where(hit, weights_ref[k : k + 1, :], weight)
    earlier = lax.broadcasted_iota(jnp.int32, (tokens, tokens), 0)
    later = lax.broadcasted_iota(jnp.int32, (tokens, tokens), 1)
    before = jnp.where(earlier < later, 1.0, 0.0).astype(jnp.bfloat16)
    rank = jnp.dot(member.astype(jnp.bfloat16), before, preferred_element_type=jnp.float32)
    return jnp.where(member > 0.0, rank, -1.0), slot, weight


def head_kernel(x_ref, routes_any, tokens_any, gate, up, down, first, rest, joined, routes_ref, tokens_ref, held, sems):
    count = gate.shape[0]
    small = [pltpu.make_async_copy(routes_any, routes_ref, sems.at[0]), pltpu.make_async_copy(tokens_any, tokens_ref, sems.at[1])]
    rows = [pl.ds(i * count, count) for i in range(3)]
    into = [pltpu.make_async_copy(v, held.at[r], sems.at[2 + i]) for i, (v, r) in enumerate(zip((gate, up, down), rows))]
    back = [pltpu.make_async_copy(held.at[r], joined.at[r], sems.at[5 + i]) for i, r in enumerate(rows)]
    for copy in small + into:
        copy.start()
    for copy in small:
        copy.wait()
    tokens = tokens_ref[...]
    rank, slot, _ = ranked(x_ref, routes_ref, SLOTS, 1)
    for step, (out, place) in enumerate(((first, 0), (first, SLOTS), (rest, 0))):
        pick = jnp.where(rank == (slot + step * SLOTS).astype(jnp.float32), 1.0, 0.0).astype(jnp.bfloat16)
        picked = jnp.dot(pick, tokens, preferred_element_type=jnp.float32).astype(jnp.bfloat16)
        chips, kinds, _, quarter = out.shape
        out[:, :, place : place + SLOTS, :] = picked.reshape(chips, kinds, SLOTS, quarter)
        into[step].wait()
        back[step].start()
    for copy in back:
        copy.wait()


def head(me, routes, tokens, weights):
    chips, (count, width) = 32, weights[0].shape
    anywhere = pl.BlockSpec(memory_space=pl.ANY)
    return pl.pallas_call(
        head_kernel,
        out_shape=[
            jax.ShapeDtypeStruct((chips, 2, CAP - SLOTS, tokens.shape[1]), tokens.dtype),
            jax.ShapeDtypeStruct((chips, 2, SLOTS, tokens.shape[1]), tokens.dtype),
            jax.ShapeDtypeStruct((3 * count, width), tokens.dtype),
        ],
        in_specs=[SMEM] + [anywhere] * 5,
        out_specs=[VMEM, VMEM, anywhere],
        scratch_shapes=[
            pltpu.VMEM(routes.shape, routes.dtype),
            pltpu.VMEM(tokens.shape, tokens.dtype),
            pltpu.VMEM((3 * count, width), tokens.dtype),
            pltpu.SemaphoreType.DMA((8,)),
        ],
        compiler_params=pltpu.CompilerParams(vmem_limit_bytes=LIMIT),
        cost_estimate=pl.CostEstimate(flops=0, bytes_accessed=14_000_000, transcendentals=0),
    )(me, routes, tokens, *weights)


def split_kernel(x_ref, both, own, other):
    own[...] = both[:, 0]
    other[...] = both[:, 1]


def weigh_kernel(x_ref, routes_ref, weights_ref, *outs):
    rank, slot, weight = ranked(x_ref, routes_ref, SLOTS, 2, weights_ref)
    for chunk, out in enumerate(outs):
        out[...] = jnp.where(rank == (slot + chunk * SLOTS).astype(jnp.float32), weight, 0.0)


def along(value, weight):
    return lax.dot_general(value, weight, (((1,), (1,)), ((), ())), preferred_element_type=jnp.float32)


def expert_kernel(chunk, x_ref, *refs):
    sources, keep, send, held, sems = refs[:6], refs[6], refs[7], refs[8:14], refs[14]
    count = sources[4].shape[0] // 3
    rows = [pl.ds(i * count, count) for i in range(3)]
    slots = pl.ds(chunk * SLOTS, SLOTS)
    pieces = [pltpu.make_async_copy(sources[i].at[:, slots, :], held[i], sems.at[i]) for i in range(4)]
    weights = []
    for half in range(2):
        for i in range(3):
            source, place = sources[4 + half].at[rows[i]], held[4 + half].at[rows[i]]
            weights.append(pltpu.make_async_copy(source, place, sems.at[4 + 3 * half + i]))
    for copy in pieces + weights:
        copy.start()
    x = x_ref[0]
    quarter = held[0].shape[2]
    blocks = (x, x ^ 1, x ^ 3, x ^ 2)

    def span(q):
        return pl.ds(pl.multiple_of(q * quarter, quarter), quarter)

    for copy in pieces:
        copy.wait()
    values = [piece[...].reshape(-1, quarter) for piece in held[:4]]
    hidden = []
    for half in range(2):
        gate, up = 0.0, 0.0
        weights[3 * half].wait()
        for value, q in zip(values, blocks):
            gate = gate + along(value, held[4 + half][rows[0], span(q)])
        weights[3 * half + 1].wait()
        for value, q in zip(values, blocks):
            up = up + along(value, held[4 + half][rows[1], span(q)])
        hidden.append((gate / (1.0 + jnp.exp(-gate)) * up).astype(jnp.bfloat16))
    weights[2].wait()
    weights[5].wait()
    for out, places in ((send, (x ^ 1, x ^ 2)), (keep, (x, x ^ 3))):
        for place, q in enumerate(places):
            total = jnp.dot(hidden[0], held[4][rows[2], span(q)], preferred_element_type=jnp.float32)
            total = total + jnp.dot(hidden[1], held[5][rows[2], span(q)], preferred_element_type=jnp.float32)
            out[:, place * quarter : (place + 1) * quarter] = total.astype(jnp.bfloat16)


def expert(me, chunk, pieces, weights):
    chips, _, quarter = pieces[0].shape
    count = chips * SLOTS
    operands = [*pieces, *weights]
    out = jax.ShapeDtypeStruct((count, 2 * quarter), jnp.bfloat16)
    held = [(chips, SLOTS, quarter)] * 4 + [v.shape for v in weights]
    return pl.pallas_call(
        functools.partial(expert_kernel, chunk),
        out_shape=[out, out],
        in_specs=[SMEM] + [pl.BlockSpec(memory_space=pl.ANY)] * len(operands),
        out_specs=[VMEM, VMEM],
        scratch_shapes=[pltpu.VMEM(v, jnp.bfloat16) for v in held] + [pltpu.SemaphoreType.DMA((10,))],
        compiler_params=pltpu.CompilerParams(vmem_limit_bytes=LIMIT),
        cost_estimate=pl.CostEstimate(flops=6 * count * 2048 * 704, bytes_accessed=24_000_000, transcendentals=0),
    )(me, *operands)


def across_rows(weight, value):
    return lax.dot_general(weight, value, (((0,), (0,)), ((), ())), preferred_element_type=jnp.float32)


def mixed(weight, value):
    high = weight.astype(jnp.bfloat16)
    low = (weight - high.astype(jnp.float32)).astype(jnp.bfloat16)
    return across_rows(high, value) + across_rows(low, value)


def mix_first_kernel(x_ref, weight, value, out):
    out[...] = mixed(weight[...], value[...])


def mix_kernel(x_ref, total, weight, value, out):
    out[...] = total[...] + mixed(weight[...], value[...])


def mix_last_kernel(x_ref, total, weight, value, keep, send):
    half = keep.shape[1]
    done = total[...] + mixed(weight[...], value[...])
    keep[...] = done[:, :half]
    send[...] = done[:, half:].astype(jnp.bfloat16)


def move_x(value, flip):
    return lax.ppermute(value, "x", [(i, i ^ flip) for i in range(4)])


def move_core(value):
    return lax.ppermute(value, "c", [(0, 1), (1, 0)])


def to_group(value):
    pairs = []
    for x in range(4):
        for core in range(2):
            stays = (x // 2) == core
            target = (x, 1 - core) if stays else (x ^ 3, core)
            pairs.append((core * 4 + x, target[1] * 4 + target[0]))
    return lax.ppermute(value, ("c", "x"), pairs)


def shards(tokens, routes, route_weights, w_gate, w_up, w_down):
    rows, quarter = tokens.shape
    routes, route_weights = routes.T, route_weights.T
    w_gate, w_up = jnp.swapaxes(w_gate, 1, 2), jnp.swapaxes(w_up, 1, 2)
    chips = 32
    me = lax.axis_index("x").astype(jnp.int32).reshape(1)
    bf16, f32 = jnp.bfloat16, jnp.float32

    def shape(*dims, dtype=bf16):
        return jax.ShapeDtypeStruct(dims, dtype)

    first, rest, joined = head(me, routes, tokens, (w_gate[0], w_up[0], w_down[0]))
    kept = to_group(joined)
    chunks = CAP // SLOTS
    mixing = call(weigh_kernel, [shape(chips * SLOTS, rows, dtype=f32)] * chunks)(me, routes, route_weights)

    def across_chips(value):
        return lax.all_to_all(value, ("y", "z"), split_axis=0, concat_axis=0, tiled=True)

    def finish(keep, received):
        return (keep.astype(f32) + received.astype(f32)).astype(bf16).reshape(chips, SLOTS, 2 * quarter)

    tie = lax.optimization_barrier
    def split(value):
        part = shape(chips, value.shape[2], quarter)
        return call(split_kernel, [part, part], moved=6_000_000)(me, value)

    own, other = split(across_chips(first))
    pieces = [own, move_x(own, 1), move_x(other, 3), move_x(other, 2)]
    rest, own = tie((rest, own))
    incoming = across_chips(rest)
    incoming, kept, pieces[1], pieces[2] = tie((incoming, kept, pieces[1], pieces[2]))
    swapped = move_core(kept)
    weights = (kept, swapped)
    own, other = split(incoming)
    later = [own, move_x(own, 1), move_x(other, 3), move_x(other, 2)]
    pieces[0], *later = tie((pieces[0], *later))
    keep0, send0 = expert(me, 0, pieces, weights)
    received0 = move_x(send0, 1)
    keep1, send1 = expert(me, 1, pieces, weights)
    keep2, send2 = expert(me, 0, later, weights)
    received0, send1, send2 = tie((received0, send1, send2))
    received1 = move_x(send1, 1)
    received1, send2 = tie((received1, send2))
    received2 = move_x(send2, 1)
    results = [finish(keep0, received0), finish(keep1, received1), finish(keep2, received2)]
    returned = [across_chips(v).reshape(-1, 2 * quarter) for v in results]
    total = call(mix_first_kernel, shape(rows, 2 * quarter, dtype=f32))(me, mixing[0], returned[0])
    total = call(mix_kernel, shape(rows, 2 * quarter, dtype=f32))(me, total, mixing[1], returned[1])
    keep, send = call(mix_last_kernel, [shape(rows, quarter, dtype=f32), shape(rows, quarter)])(
        me, total, mixing[2], returned[2]
    )
    return (keep + move_x(send, 3).astype(f32)).astype(bf16)


def solution(mesh):
    fine = Mesh(mesh.devices.reshape(4, 8, 2, 4), ("y", "z", "c", "x"))
    expert = ("y", "z", "c")
    placed = (
        P(expert, "x"),
        P(expert, None),
        P(expert, None),
        P(expert, None, "x"),
        P(expert, None, "x"),
        P(expert, "x", None),
    )
    return jax.shard_map(shards, mesh=fine, in_specs=placed, out_specs=P(expert, "x"), check_vma=False)
```

time: 223 us -> 198 us (0.89)
  blocking collectives: 0 us -> 40.2 us
  starting transfers between devices: 82.4 us -> 43.7 us
  waiting for transfers between devices: 102 us -> 81.6 us
  local copies, waits for them, and re-layouts: 9 us -> 0.91 us
  other arithmetic: 0.68 us -> 3.7 us
    all_to_all x0 -> x1, blocking collectives: none -> 40.2 us  [across_chips(): lax.all_to_all(value, ('y', 'z'), split_axis=0, concat_axis=0, tiled=True)]
    all_to_all x6 -> x4, starting transfers between devices: 58.5 us -> 27.1 us  [across_chips(): lax.all_to_all(value, ('y', 'z'), split_axis=0, concat_axis=0, tiled=True)]
    ppermute x3 -> x1, waiting for transfers between devices: 9.86 us -> 0.01 us  [to_group(): return lax.ppermute(value, ('c', 'x'), pairs)]
    all_to_all x6 -> x4, waiting for transfers between devices: 30.1 us -> 22.2 us  [across_chips(): lax.all_to_all(value, ('y', 'z'), split_axis=0, concat_axis=0, tiled=True)]
    unnamed x32 -> x28, local copies, waits for them, and re-layouts: 5.06 us -> 0.91 us
    reshape x3 -> x0, local copies, waits for them, and re-layouts: 3.94 us -> none  [shards(): other = incoming[:, SLOTS:].reshape(at, quarter)]
    ppermute x14 -> x10, starting transfers between devices: 20.3 us -> 16.5 us  [move_x(): return lax.ppermute(value, 'x', [(i, i ^ flip) for i in range(4)])]
    reshape x0 -> x3, other arithmetic: none -> 3.01 us  [finish(): (keep.astype(f32) + received.astype(f32)).astype(bf16)]
  transfers between devices with their start and end apart: 27 -> 16, of which waited for: 15 -> 12; matrix products, arithmetic and copies ran while one was open for 2% -> 1% of each run, Pallas kernels for 13% -> 7%
where the time goes in v2:
time: 198 us; the launch traced here: 197 us
  waiting for transfers between devices  81.6 us (41%)
  starting transfers between devices  43.7 us (22%)
  blocking collectives  40.2 us (20%)
  Pallas kernels  26.5 us (13%)
  other arithmetic  3.7 us (2%)
    ppermute x10, waiting for transfers between devices, move_x(): return lax.ppermute(value, 'x', [(i, i ^ flip) for i in range(4)])  59.4 us
    all_to_all x1, blocking collectives, across_chips(): lax.all_to_all(value, ('y', 'z'), split_axis=0, concat_axis=0, tiled=True)  40.2 us
    all_to_all x4, starting transfers between devices, across_chips(): lax.all_to_all(value, ('y', 'z'), split_axis=0, concat_axis=0, tiled=True)  27.1 us
    all_to_all x4, waiting for transfers between devices, across_chips(): lax.all_to_all(value, ('y', 'z'), split_axis=0, concat_axis=0, tiled=True)  22.2 us
    pallas_call x3, Pallas kernels, expert(): pl.pallas_call(functools.partial(expert_kernel, chunk), out_shape=[out, o...  20.4 us
    ppermute x10, starting transfers between devices, move_x(): return lax.ppermute(value, 'x', [(i, i ^ flip) for i in range(4)])  16.5 us
    pallas_call x1, Pallas kernels, head(): pl.pallas_call(head_kernel, out_shape=[jax.ShapeDtypeStruct((chips, 2, CA...  4.72 us
  transfers between devices with their start and end apart: 16, of which 12 were waited for; matrix products, arithmetic and copies ran while one was open for 1% of the time, Pallas kernels for 7%

profile of v2, /device:TPU:32, one launch (start us, length us, event | category | flops | bytes accessed | tf_op | source)
XLA Modules:
  0.0 196.9 jit_solution(15466436348284672233)
XLA Ops:
  0.0 4.7 %shard_map.65 = (bf16[32,2,16,512]{3,2,1,0:T(8,128)(2,1)}, bf16[32,2,8,512]{3,2,1,0:T(8,128)(2,1)}, bf16[1056,2048]{1,0:T(8,128)(2,1)}) custom-call(s32[1]{0:T(128)} %bitcast.x_ref, s32[6,128]{1,0:T(8,128)} %bitcast.22, bf16[128,512]{1,0:T(8,128)(2,1)} %tokens_any.1, bf16[352,2048]{1,0:T(8,128)(2,1)} %bitcast.25, bf16[352,2048]{1,0:T(8,128)(2,1)} %bitcast.26, ...), custom_call_target="tpu_custom_call" | custom-call | bytes 14000000 | tf_op jit(solution)/shard_map/pallas_call | solution.py:80
  4.8 40.2 %all_to_all.25.both = bf16[32,2,16,512]{3,2,1,0:T(8,128)(2,1)S(1)} all-to-all(bf16[32,2,16,512]{3,2,1,0:T(8,128)(2,1)} %get-tuple-element.39), channel_id=1, replica_groups=mesh['y'=4,'z'=8,'c'=2,'x'=4] {'y','z'}, dimensions={0} | all-to-all | bytes 2097152 | tf_op jit(solution)/shard_map/all_to_all | solution.py:234
  45.1 5.6 %all-to-all-start.1 = ((bf16[32,2,8,512]{3,2,1,0:T(8,128)(2,1)}), bf16[32,2,8,512]{3,2,1,0:T(8,128)(2,1)S(1)}, u32[]{:S(2)}, u32[]{:S(2)}) async-start(bf16[32,2,8,512]{3,2,1,0:T(8,128)(2,1)} %get-tuple-element.42), calls=%async_computation.1 | async-start | bytes 1048576 | tf_op jit(solution)/shard_map/all_to_all | solution.py:234
  50.7 2.1 %collective-permute-start.1 = (bf16[32,16,512]{2,1,0:T(8,128)(2,1)S(1)}, bf16[32,16,512]{2,1,0:T(8,128)(2,1)S(1)}, u32[]{:S(2)}, u32[]{:S(2)}) collective-permute-start(bf16[32,16,512]{2,1,0:T(8,128)(2,1)S(1)} %get-tuple-element.48.refs_0_), channel_id=1, source_target_pairs={{0,1},{1,0},{2,3},{3,2},{4,5},{5,4},{6,7},{7,6},{8,9},{9,8},{10,11... | collective-permute-start | bytes 1572872 | tf_op jit(solution)/shard_map/ppermute | solution.py:200
  52.8 1.6 collective-permute-start.2
  54.3 10.3 %collective-permute-done.1.refs_1_ = bf16[32,16,512]{2,1,0:T(8,128)(2,1)S(1)} collective-permute-done((bf16[32,16,512]{2,1,0:T(8,128)(2,1)S(1)}, bf16[32,16,512]{2,1,0:T(8,128)(2,1)S(1)}, u32[]{:S(2)}, u32[]{:S(2)}) %collective-permute-start.1) | collective-permute-done | bytes 524320 | tf_op jit(solution)/shard_map/ppermute | solution.py:200
  64.6 2.8 %collective-permute-done.2.refs_2_ = bf16[32,16,512]{2,1,0:T(8,128)(2,1)S(1)} collective-permute-done((bf16[32,16,512]{2,1,0:T(8,128)(2,1)S(1)}, bf16[32,16,512]{2,1,0:T(8,128)(2,1)S(1)}, u32[]{:S(2)}, u32[]{:S(2)}) %collective-permute-start.2) | collective-permute-done | bytes 524320 | tf_op jit(solution)/shard_map/ppermute | solution.py:200
  67.4 1.7 all-to-all-done.1.both
  69.1 1.7 collective-permute-start.6
  71.6 1.9 collective-permute-start.4
  73.5 1.6 collective-permute-start.5
  75.1 14.7 %collective-permute-done.3.refs_1_ = bf16[32,8,512]{2,1,0:T(8,128)(2,1)S(1)} collective-permute-done((bf16[32,8,512]{2,1,0:T(8,128)(2,1)S(1)}, bf16[32,8,512]{2,1,0:T(8,128)(2,1)S(1)}, u32[]{:S(2)}, u32[]{:S(2)}) %collective-permute-start.3) | collective-permute-done | bytes 262176 | tf_op jit(solution)/shard_map/ppermute | solution.py:200
  89.8 1.1 collective-permute-done.4.refs_2_
  90.9 5.3 %collective-permute-done.5.refs_3_ = bf16[32,8,512]{2,1,0:T(8,128)(2,1)S(1)} collective-permute-done((bf16[32,8,512]{2,1,0:T(8,128)(2,1)S(1)}, bf16[32,8,512]{2,1,0:T(8,128)(2,1)S(1)}, u32[]{:S(2)}, u32[]{:S(2)}) %collective-permute-start.5) | collective-permute-done | bytes 262176 | tf_op jit(solution)/shard_map/ppermute | solution.py:200
  97.1 6.8 %shard_map.68 = (bf16[256,1024]{1,0:T(8,128)(2,1)}, bf16[256,1024]{1,0:T(8,128)(2,1)}) custom-call(s32[1]{0:T(128)} %bitcast.x_ref, bf16[32,16,512]{2,1,0:T(8,128)(2,1)} %copy-done, bf16[32,16,512]{2,1,0:T(8,128)(2,1)} %copy-done.4, bf16[32,16,512]{2,1,0:T(8,128)(2,1)} %copy-done.5, bf16[32,16,512]{2,1,0:T(8,128)(2,1)} %copy-done.6, ...), custom_call_target="tpu_custom_call" | custom-call | flops 2214592512 | bytes 24000000 | tf_op jit(solution)/shard_map/pallas_call | solution.py:163
  103.9 1.7 collective-permute-start.8
  105.6 6.8 %shard_map.69 = (bf16[256,1024]{1,0:T(8,128)(2,1)}, bf16[256,1024]{1,0:T(8,128)(2,1)}) custom-call(s32[1]{0:T(128)} %bitcast.x_ref, bf16[32,16,512]{2,1,0:T(8,128)(2,1)} %copy-done, bf16[32,16,512]{2,1,0:T(8,128)(2,1)} %copy-done.4, bf16[32,16,512]{2,1,0:T(8,128)(2,1)} %copy-done.5, bf16[32,16,512]{2,1,0:T(8,128)(2,1)} %copy-done.6, ...), custom_call_target="tpu_custom_call" | custom-call | flops 2214592512 | bytes 24000000 | tf_op jit(solution)/shard_map/pallas_call | solution.py:163
  112.5 6.8 %shard_map.70 = (bf16[256,1024]{1,0:T(8,128)(2,1)}, bf16[256,1024]{1,0:T(8,128)(2,1)}) custom-call(s32[1]{0:T(128)} %bitcast.x_ref, bf16[32,8,512]{2,1,0:T(8,128)(2,1)} %copy-done.1, bf16[32,8,512]{2,1,0:T(8,128)(2,1)} %copy-done.10, bf16[32,8,512]{2,1,0:T(8,128)(2,1)} %copy-done.11, bf16[32,8,512]{2,1,0:T(8,128)(2,1)} %copy-done.12, ...), custom_call_target="tpu_custom_call" | custom-call | flops 2214592512 | bytes 24000000 | tf_op jit(solution)/shard_map/pallas_call | solution.py:163
  119.4 1.0 fusion
  120.4 8.6 %all-to-all-start.2 = ((bf16[32,8,1024]{2,1,0:T(8,128)(2,1)}), bf16[32,8,1024]{2,1,0:T(8,128)(2,1)S(1)}, u32[]{:S(2)}, u32[]{:S(2)}) async-start(bf16[32,8,1024]{2,1,0:T(8,128)(2,1)} %fusion), calls=%async_computation.2 | async-start | bytes 1048576 | tf_op jit(solution)/shard_map/all_to_all | solution.py:234
  129.0 1.8 collective-permute-start.9
  130.8 11.1 %collective-permute-done.9 = bf16[256,1024]{1,0:T(8,128)(2,1)S(1)} collective-permute-done((bf16[256,1024]{1,0:T(8,128)(2,1)}, bf16[256,1024]{1,0:T(8,128)(2,1)S(1)}, u32[]{:S(2)}, u32[]{:S(2)}) %collective-permute-start.9) | collective-permute-done | bytes 524320 | tf_op jit(solution)/shard_map/ppermute | solution.py:200
  142.9 3.2 %all-to-all-done.2 = bf16[32,8,1024]{2,1,0:T(8,128)(2,1)S(1)} async-done(((bf16[32,8,1024]{2,1,0:T(8,128)(2,1)}), bf16[32,8,1024]{2,1,0:T(8,128)(2,1)S(1)}, u32[]{:S(2)}, u32[]{:S(2)}) %all-to-all-start.2) | async-done | bytes 524320 | tf_op jit(solution)/shard_map/all_to_all | solution.py:234
  146.2 6.5 %all-to-all-start.3 = ((bf16[32,8,1024]{2,1,0:T(8,128)(2,1)}), bf16[32,8,1024]{2,1,0:T(8,128)(2,1)S(1)}, u32[]{:S(2)}, u32[]{:S(2)}) async-start(bf16[32,8,1024]{2,1,0:T(8,128)(2,1)} %fusion.1), calls=%async_computation.3 | async-start | bytes 1048576 | tf_op jit(solution)/shard_map/all_to_all | solution.py:234
  152.7 1.8 collective-permute-start.10
  154.6 9.4 %collective-permute-done.10 = bf16[256,1024]{1,0:T(8,128)(2,1)S(1)} collective-permute-done((bf16[256,1024]{1,0:T(8,128)(2,1)S(1)}, bf16[256,1024]{1,0:T(8,128)(2,1)S(1)}, u32[]{:S(2)}, u32[]{:S(2)}) %collective-permute-start.10) | collective-permute-done | bytes 524320 | tf_op jit(solution)/shard_map/ppermute | solution.py:200
  164.0 1.0 fusion.2
  165.0 3.4 %all-to-all-done.3 = bf16[32,8,1024]{2,1,0:T(8,128)(2,1)S(1)} async-done(((bf16[32,8,1024]{2,1,0:T(8,128)(2,1)}), bf16[32,8,1024]{2,1,0:T(8,128)(2,1)S(1)}, u32[]{:S(2)}, u32[]{:S(2)}) %all-to-all-start.3) | async-done | bytes 524320 | tf_op jit(solution)/shard_map/all_to_all | solution.py:234
  168.4 6.4 %all-to-all-start.4 = ((bf16[32,8,1024]{2,1,0:T(8,128)(2,1)}), bf16[32,8,1024]{2,1,0:T(8,128)(2,1)S(1)}, u32[]{:S(2)}, u32[]{:S(2)}) async-start(bf16[32,8,1024]{2,1,0:T(8,128)(2,1)} %fusion.2), calls=%async_computation.4 | async-start | bytes 1048576 | tf_op jit(solution)/shard_map/all_to_all | solution.py:234
  175.7 13.8 %all-to-all-done.4 = bf16[32,8,1024]{2,1,0:T(8,128)(2,1)S(1)} async-done(((bf16[32,8,1024]{2,1,0:T(8,128)(2,1)}), bf16[32,8,1024]{2,1,0:T(8,128)(2,1)S(1)}, u32[]{:S(2)}, u32[]{:S(2)}) %all-to-all-start.4) | async-done | bytes 524320 | tf_op jit(solution)/shard_map/all_to_all | solution.py:234
  189.9 1.6 collective-permute-start.11
  191.5 4.6 %collective-permute-done.11 = bf16[128,512]{1,0:T(8,128)(2,1)S(1)} collective-permute-done((bf16[128,512]{1,0:T(8,128)(2,1)S(1)}, bf16[128,512]{1,0:T(8,128)(2,1)S(1)}, u32[]{:S(2)}, u32[]{:S(2)}) %collective-permute-start.11) | collective-permute-done | bytes 131104 | tf_op jit(solution)/shard_map/ppermute | solution.py:200
  (43 shorter events, 4.7 us)
Async XLA Ops:
  4.7 64.4 %collective-permute-start = (bf16[1056,2048]{1,0:T(8,128)(2,1)}, bf16[1056,2048]{1,0:T(8,128)(2,1)}, u32[]{:S(2)}, u32[]{:S(2)}) collective-permute-start(bf16[1056,2048]{1,0:T(8,128)(2,1)} %get-tuple-element.43), channel_id=1, source_target_pairs={{0,4},{4,7},{1,5},{5,6},{2,1},{6,2},{3,0},{7,3},{8,12},{12,15},{9,... | collective-permute-start | bytes 12976136 | tf_op jit(solution)/shard_map/ppermute | solution.py:214
  45.1 51.2 %copy-start = (bf16[32,16,512]{2,1,0:T(8,128)(2,1)}, bf16[32,16,512]{2,1,0:T(8,128)(2,1)S(1)}, u32[]{:S(2)}) copy-start(bf16[32,16,512]{2,1,0:T(8,128)(2,1)S(1)} %get-tuple-element.48.refs_0_) | copy-start | bytes 1572868
  45.1 24.0 %all-to-all-start.1 = ((bf16[32,2,8,512]{3,2,1,0:T(8,128)(2,1)}), bf16[32,2,8,512]{3,2,1,0:T(8,128)(2,1)S(1)}, u32[]{:S(2)}, u32[]{:S(2)}) async-start(bf16[32,2,8,512]{3,2,1,0:T(8,128)(2,1)} %get-tuple-element.42), calls=%async_computation.1 | async-start | bytes 1048576 | tf_op jit(solution)/shard_map/all_to_all | solution.py:234
  50.7 13.9 %collective-permute-start.1 = (bf16[32,16,512]{2,1,0:T(8,128)(2,1)S(1)}, bf16[32,16,512]{2,1,0:T(8,128)(2,1)S(1)}, u32[]{:S(2)}, u32[]{:S(2)}) collective-permute-start(bf16[32,16,512]{2,1,0:T(8,128)(2,1)S(1)} %get-tuple-element.48.refs_0_), channel_id=1, source_target_pairs={{0,1},{1,0},{2,3},{3,2},{4,5},{5,4},{6,7},{7,6},{8,9},{9,8},{10,11... | collective-permute-start | bytes 1572872 | tf_op jit(solution)/shard_map/ppermute | solution.py:200
  52.8 14.6 %collective-permute-start.2 = (bf16[32,16,512]{2,1,0:T(8,128)(2,1)S(1)}, bf16[32,16,512]{2,1,0:T(8,128)(2,1)S(1)}, u32[]{:S(2)}, u32[]{:S(2)}) collective-permute-start(bf16[32,16,512]{2,1,0:T(8,128)(2,1)S(1)} %get-tuple-element.44), channel_id=1, source_target_pairs={{0,3},{1,2},{2,1},{3,0},{4,7},{5,6},{6,5},{7,4},{8,11},{9,10},{10,... | collective-permute-start | bytes 1572872 | tf_op jit(solution)/shard_map/ppermute | solution.py:200
  64.6 31.7 %copy-start.4 = (bf16[32,16,512]{2,1,0:T(8,128)(2,1)}, bf16[32,16,512]{2,1,0:T(8,128)(2,1)S(1)}, u32[]{:S(2)}) copy-start(bf16[32,16,512]{2,1,0:T(8,128)(2,1)S(1)} %collective-permute-done.1.refs_1_) | copy-start | bytes 1572868
  67.4 28.9 %copy-start.5 = (bf16[32,16,512]{2,1,0:T(8,128)(2,1)}, bf16[32,16,512]{2,1,0:T(8,128)(2,1)S(1)}, u32[]{:S(2)}) copy-start(bf16[32,16,512]{2,1,0:T(8,128)(2,1)S(1)} %collective-permute-done.2.refs_2_) | copy-start | bytes 1572868
  69.1 27.1 %collective-permute-start.7 = (bf16[1056,2048]{1,0:T(8,128)(2,1)}, bf16[1056,2048]{1,0:T(8,128)(2,1)}, u32[]{:S(2)}, u32[]{:S(2)}) collective-permute-start(bf16[1056,2048]{1,0:T(8,128)(2,1)} %collective-permute-done.refs_4_), channel_id=1, source_target_pairs={{0,4},{4,0},{1,5},{5,1},{2,6},{6,2},{3,7},{7,3},{8,12},{12,8},{9,1... | collective-permute-start | bytes 12976136 | tf_op jit(solution)/shard_map/ppermute | solution.py:204
  69.1 27.1 %collective-permute-start.6 = (bf16[32,16,512]{2,1,0:T(8,128)(2,1)S(1)}, bf16[32,16,512]{2,1,0:T(8,128)(2,1)S(1)}, u32[]{:S(2)}, u32[]{:S(2)}) collective-permute-start(bf16[32,16,512]{2,1,0:T(8,128)(2,1)S(1)} %get-tuple-element.44), channel_id=1, source_target_pairs={{0,2},{1,3},{2,0},{3,1},{4,6},{5,7},{6,4},{7,5},{8,10},{9,11},{10,... | collective-permute-start | bytes 1572872 | tf_op jit(solution)/shard_map/ppermute | solution.py:200
  70.9 33.1 %copy-start.1 = (bf16[32,8,512]{2,1,0:T(8,128)(2,1)}, bf16[32,8,512]{2,1,0:T(8,128)(2,1)S(1)}, u32[]{:S(2)}) copy-start(bf16[32,8,512]{2,1,0:T(8,128)(2,1)S(1)} %get-tuple-element.55.refs_0_) | copy-start | bytes 786436
  70.9 18.9 %collective-permute-start.3 = (bf16[32,8,512]{2,1,0:T(8,128)(2,1)S(1)}, bf16[32,8,512]{2,1,0:T(8,128)(2,1)S(1)}, u32[]{:S(2)}, u32[]{:S(2)}) collective-permute-start(bf16[32,8,512]{2,1,0:T(8,128)(2,1)S(1)} %get-tuple-element.55.refs_0_), channel_id=1, source_target_pairs={{0,1},{1,0},{2,3},{3,2},{4,5},{5,4},{6,7},{7,6},{8,9},{9,8},{10,11... | collective-permute-start | bytes 786440 | tf_op jit(solution)/shard_map/ppermute | solution.py:200
  71.6 19.4 %collective-permute-start.4 = (bf16[32,8,512]{2,1,0:T(8,128)(2,1)S(1)}, bf16[32,8,512]{2,1,0:T(8,128)(2,1)S(1)}, u32[]{:S(2)}, u32[]{:S(2)}) collective-permute-start(bf16[32,8,512]{2,1,0:T(8,128)(2,1)S(1)} %get-tuple-element.47), channel_id=1, source_target_pairs={{0,3},{1,2},{2,1},{3,0},{4,7},{5,6},{6,5},{7,4},{8,11},{9,10},{10,... | collective-permute-start | bytes 786440 | tf_op jit(solution)/shard_map/ppermute | solution.py:200
  73.5 22.8 %collective-permute-start.5 = (bf16[32,8,512]{2,1,0:T(8,128)(2,1)S(1)}, bf16[32,8,512]{2,1,0:T(8,128)(2,1)S(1)}, u32[]{:S(2)}, u32[]{:S(2)}) collective-permute-start(bf16[32,8,512]{2,1,0:T(8,128)(2,1)S(1)} %get-tuple-element.47), channel_id=1, source_target_pairs={{0,2},{1,3},{2,0},{3,1},{4,6},{5,7},{6,4},{7,5},{8,10},{9,11},{10,... | collective-permute-start | bytes 786440 | tf_op jit(solution)/shard_map/ppermute | solution.py:200
  89.8 22.7 %copy-start.10 = (bf16[32,8,512]{2,1,0:T(8,128)(2,1)}, bf16[32,8,512]{2,1,0:T(8,128)(2,1)S(1)}, u32[]{:S(2)}) copy-start(bf16[32,8,512]{2,1,0:T(8,128)(2,1)S(1)} %collective-permute-done.3.refs_1_) | copy-start | bytes 786436
  90.9 21.5 %copy-start.11 = (bf16[32,8,512]{2,1,0:T(8,128)(2,1)}, bf16[32,8,512]{2,1,0:T(8,128)(2,1)S(1)}, u32[]{:S(2)}) copy-start(bf16[32,8,512]{2,1,0:T(8,128)(2,1)S(1)} %collective-permute-done.4.refs_2_) | copy-start | bytes 786436
  96.2 16.2 %copy-start.12 = (bf16[32,8,512]{2,1,0:T(8,128)(2,1)}, bf16[32,8,512]{2,1,0:T(8,128)(2,1)S(1)}, u32[]{:S(2)}) copy-start(bf16[32,8,512]{2,1,0:T(8,128)(2,1)S(1)} %collective-permute-done.5.refs_3_) | copy-start | bytes 786436
  96.2 0.9 copy-start.6
  103.9 15.4 %collective-permute-start.8 = (bf16[256,1024]{1,0:T(8,128)(2,1)}, bf16[256,1024]{1,0:T(8,128)(2,1)S(1)}, u32[]{:S(2)}, u32[]{:S(2)}) collective-permute-start(bf16[256,1024]{1,0:T(8,128)(2,1)} %get-tuple-element.53), channel_id=1, source_target_pairs={{0,1},{1,0},{2,3},{3,2},{4,5},{5,4},{6,7},{7,6},{8,9},{9,8},{10,11... | collective-permute-start | bytes 1572872 | tf_op jit(solution)/shard_map/ppermute | solution.py:200
  112.5 6.9 %copy-start.9 = (bf16[256,1024]{1,0:T(8,128)(2,1)S(1)}, bf16[256,1024]{1,0:T(8,128)(2,1)}, u32[]{:S(2)}) copy-start(bf16[256,1024]{1,0:T(8,128)(2,1)} %get-tuple-element.52) | copy-start | bytes 1572868
  112.5 29.5 %copy-start.8 = (bf16[256,1024]{1,0:T(8,128)(2,1)S(1)}, bf16[256,1024]{1,0:T(8,128)(2,1)}, u32[]{:S(2)}) copy-start(bf16[256,1024]{1,0:T(8,128)(2,1)} %get-tuple-element.62) | copy-start | bytes 1572868
  119.3 33.4 %copy-start.13 = (bf16[256,1024]{1,0:T(8,128)(2,1)S(1)}, bf16[256,1024]{1,0:T(8,128)(2,1)}, u32[]{:S(2)}) copy-start(bf16[256,1024]{1,0:T(8,128)(2,1)} %get-tuple-element.68) | copy-start | bytes 1572868
  119.3 44.7 %copy-start.7 = (bf16[256,1024]{1,0:T(8,128)(2,1)S(1)}, bf16[256,1024]{1,0:T(8,128)(2,1)}, u32[]{:S(2)}) copy-start(bf16[256,1024]{1,0:T(8,128)(2,1)} %get-tuple-element.67) | copy-start | bytes 1572868
  119.3 55.5 %copy-start.2 = (s32[128,6]{0,1:T(8,128)S(1)}, s32[128,6]{0,1:T(8,128)}, u32[]{:S(2)}) copy-start(s32[128,6]{0,1:T(8,128)} %param.7) | copy-start | bytes 9220
  119.4 55.5 %copy-start.3 = (f32[128,6]{0,1:T(8,128)S(1)}, f32[128,6]{0,1:T(8,128)}, u32[]{:S(2)}) copy-start(f32[128,6]{0,1:T(8,128)} %param.8) | copy-start | bytes 9220
  120.4 25.8 %all-to-all-start.2 = ((bf16[32,8,1024]{2,1,0:T(8,128)(2,1)}), bf16[32,8,1024]{2,1,0:T(8,128)(2,1)S(1)}, u32[]{:S(2)}, u32[]{:S(2)}) async-start(bf16[32,8,1024]{2,1,0:T(8,128)(2,1)} %fusion), calls=%async_computation.2 | async-start | bytes 1048576 | tf_op jit(solution)/shard_map/all_to_all | solution.py:234
  129.0 12.9 %collective-permute-start.9 = (bf16[256,1024]{1,0:T(8,128)(2,1)}, bf16[256,1024]{1,0:T(8,128)(2,1)S(1)}, u32[]{:S(2)}, u32[]{:S(2)}) collective-permute-start(bf16[256,1024]{1,0:T(8,128)(2,1)} %get-tuple-element.63), channel_id=1, source_target_pairs={{0,1},{1,0},{2,3},{3,2},{4,5},{5,4},{6,7},{7,6},{8,9},{9,8},{10,11... | collective-permute-start | bytes 1572872 | tf_op jit(solution)/shard_map/ppermute | solution.py:200
  146.2 22.2 %all-to-all-start.3 = ((bf16[32,8,1024]{2,1,0:T(8,128)(2,1)}), bf16[32,8,1024]{2,1,0:T(8,128)(2,1)S(1)}, u32[]{:S(2)}, u32[]{:S(2)}) async-start(bf16[32,8,1024]{2,1,0:T(8,128)(2,1)} %fusion.1), calls=%async_computation.3 | async-start | bytes 1048576 | tf_op jit(solution)/shard_map/all_to_all | solution.py:234
  152.7 11.3 %collective-permute-start.10 = (bf16[256,1024]{1,0:T(8,128)(2,1)S(1)}, bf16[256,1024]{1,0:T(8,128)(2,1)S(1)}, u32[]{:S(2)}, u32[]{:S(2)}) collective-permute-start(bf16[256,1024]{1,0:T(8,128)(2,1)S(1)} %copy-done.13), channel_id=1, source_target_pairs={{0,1},{1,0},{2,3},{3,2},{4,5},{5,4},{6,7},{7,6},{8,9},{9,8},{10,11... | collective-permute-start | bytes 1572872 | tf_op jit(solution)/shard_map/ppermute | solution.py:200
  168.4 21.2 %all-to-all-start.4 = ((bf16[32,8,1024]{2,1,0:T(8,128)(2,1)}), bf16[32,8,1024]{2,1,0:T(8,128)(2,1)S(1)}, u32[]{:S(2)}, u32[]{:S(2)}) async-start(bf16[32,8,1024]{2,1,0:T(8,128)(2,1)} %fusion.2), calls=%async_computation.4 | async-start | bytes 1048576 | tf_op jit(solution)/shard_map/all_to_all | solution.py:234
  189.9 6.3 %collective-permute-start.11 = (bf16[128,512]{1,0:T(8,128)(2,1)S(1)}, bf16[128,512]{1,0:T(8,128)(2,1)S(1)}, u32[]{:S(2)}, u32[]{:S(2)}) collective-permute-start(bf16[128,512]{1,0:T(8,128)(2,1)S(1)} %get-tuple-element.70), channel_id=1, source_target_pairs={{0,3},{1,2},{2,1},{3,0},{4,7},{5,6},{6,5},{7,4},{8,11},{9,10},{10,... | collective-permute-start | bytes 393224 | tf_op jit(solution)/shard_map/ppermute | solution.py:200

commit v3 on v2

v3 whole, which is shorter than its diff:
```python
import jax
import jax.numpy as jnp
from jax import lax
from jax.experimental import pallas as pl
from jax.experimental.pallas import tpu as pltpu
from jax.sharding import Mesh
from jax.sharding import PartitionSpec as P

SLOTS = 8
CAP = 24
VMEM = pl.BlockSpec(memory_space=pltpu.VMEM)
SMEM = pl.BlockSpec(memory_space=pltpu.SMEM)
LIMIT = 60 * 1024 * 1024


def call(kernel, outs, flops=0, moved=0):
    def run(*args):
        return pl.pallas_call(
            kernel,
            out_shape=outs,
            in_specs=[SMEM] + [VMEM] * (len(args) - 1),
            out_specs=jax.tree.map(lambda _: VMEM, outs),
            compiler_params=pltpu.CompilerParams(vmem_limit_bytes=16 * 1024 * 1024),
            cost_estimate=pl.CostEstimate(flops=flops, bytes_accessed=moved, transcendentals=0),
        )(*args)

    return run


def expert_order():
    x, core = lax.axis_index("x"), lax.axis_index("c")
    return jnp.where(core == 0, x // 2, 1 - ((x + 1) // 2) % 2).astype(jnp.int32)


def ranked(routes_ref, slots, step, weights_ref=None):
    tokens = routes_ref.shape[1]
    lanes = 64 // step * slots
    swap = expert_order()
    rows = lax.broadcasted_iota(jnp.int32, (lanes, tokens), 0)
    named, slot = (rows // slots) * step, rows % slots
    routes = routes_ref[...] ^ swap
    member = jnp.zeros((lanes, tokens), jnp.float32)
    weight = jnp.zeros((lanes, tokens), jnp.float32)
    for k in range(routes.shape[0]):
        hit = routes[k : k + 1, :] == named
        member = jnp.where(hit, 1.0, member)
        if weights_ref is not None:
            weight = jnp.where(hit, weights_ref[k : k + 1, :], weight)
    earlier = lax.broadcasted_iota(jnp.int32, (tokens, tokens), 0)
    later = lax.broadcasted_iota(jnp.int32, (tokens, tokens), 1)
    before = jnp.where(earlier < later, 1.0, 0.0).astype(jnp.bfloat16)
    rank = jnp.dot(member.astype(jnp.bfloat16), before, preferred_element_type=jnp.float32)
    return jnp.where(member > 0.0, rank, -1.0), slot, weight


def head_kernel(routes_any, tokens_any, gate, up, down, out, joined, routes_ref, tokens_ref, held, sems):
    count = gate.shape[0]
    small = [pltpu.make_async_copy(routes_any, routes_ref, sems.at[0]), pltpu.make_async_copy(tokens_any, tokens_ref, sems.at[1])]
    rows = [pl.ds(i * count, count) for i in range(3)]
    into = [pltpu.make_async_copy(v, held.at[r], sems.at[2 + i]) for i, (v, r) in enumerate(zip((gate, up, down), rows))]
    back = [pltpu.make_async_copy(held.at[r], joined.at[r], sems.at[5 + i]) for i, r in enumerate(rows)]
    for copy in small + into:
        copy.start()
    for copy in small:
        copy.wait()
    tokens = tokens_ref[...]
    rank, slot, _ = ranked(routes_ref, SLOTS, 1)
    chips, kinds, _, quarter = out.shape
    for step in range(3):
        pick = jnp.where(rank == (slot + step * SLOTS).astype(jnp.float32), 1.0, 0.0).astype(jnp.bfloat16)
        picked = jnp.dot(pick, tokens, preferred_element_type=jnp.float32).astype(jnp.bfloat16)
        out[:, :, step * SLOTS : (step + 1) * SLOTS, :] = picked.reshape(chips, kinds, SLOTS, quarter)
        into[step].wait()
        back[step].start()
    for copy in back:
        copy.wait()


def head(routes, tokens, weights):
    chips, (count, width) = 32, weights[0].shape
    anywhere = pl.BlockSpec(memory_space=pl.ANY)
    return pl.pallas_call(
        head_kernel,
        out_shape=[
            jax.ShapeDtypeStruct((chips, 2, CAP, tokens.shape[1]), tokens.dtype),
            jax.ShapeDtypeStruct((3 * count, width), tokens.dtype),
        ],
        in_specs=[anywhere] * 5,
        out_specs=[VMEM, anywhere],
        scratch_shapes=[
            pltpu.VMEM(routes.shape, routes.dtype),
            pltpu.VMEM(tokens.shape, tokens.dtype),
            pltpu.VMEM((3 * count, width), tokens.dtype),
            pltpu.SemaphoreType.DMA((8,)),
        ],
        compiler_params=pltpu.CompilerParams(vmem_limit_bytes=LIMIT),
        cost_estimate=pl.CostEstimate(flops=0, bytes_accessed=14_000_000, transcendentals=0),
    )(routes, tokens, *weights)


def split_kernel(x_ref, both, *outs):
    first = 0
    for own, other in (outs[:2], outs[2:]):
        count = own.shape[1]
        own[...] = both[:, 0, first : first + count, :]
        other[...] = both[:, 1, first : first + count, :]
        first += count


def weigh_kernel(x_ref, routes_ref, weights_ref, *outs):
    first = 0
    for out in outs:
        slots = out.shape[0] // 32
        rank, slot, weight = ranked(routes_ref, slots, 2, weights_ref)
        out[...] = jnp.where(rank == (slot + first).astype(jnp.float32), weight, 0.0)
        first += slots


def along(value, weight):
    return lax.dot_general(value, weight, (((1,), (1,)), ((), ())), preferred_element_type=jnp.float32)


def expert_kernel(x_ref, *refs):
    sources, (local, moved, crossed), keep, send, held, sems = refs[:4], refs[4:7], refs[7], refs[8], refs[9:15], refs[15]
    count = local.shape[0] // 3
    rows = [pl.ds(i * count, count) for i in range(3)]
    pieces = [pltpu.make_async_copy(sources[i], held[i], sems.at[i]) for i in range(4)]

    def weight(source, half, i):
        return pltpu.make_async_copy(source.at[rows[i]], held[4 + half].at[rows[i]], sems.at[4 + 3 * half + i])

    for copy in pieces:
        copy.start()
    for half, flag, yes, no in ((0, x_ref[4], local, moved), (1, x_ref[5], moved, crossed)):

        @pl.when(flag == 1)
        def _():
            for i in range(3):
                weight(yes, half, i).start()

        @pl.when(flag == 0)
        def _():
            for i in range(3):
                weight(no, half, i).start()

    weights = [weight(local, half, i) for half in range(2) for i in range(3)]
    quarter = held[0].shape[2]
    x, partner, far, across = (x_ref[i] for i in range(4))
    blocks = (x, partner, far, across)

    def span(q):
        return pl.ds(pl.multiple_of(q * quarter, quarter), quarter)

    for copy in pieces:
        copy.wait()
    values = [piece[...].reshape(-1, quarter) for piece in held[:4]]
    hidden = []
    for half in range(2):
        gate, up = 0.0, 0.0
        weights[3 * half].wait()
        for value, q in zip(values, blocks):
            gate = gate + along(value, held[4 + half][rows[0], span(q)])
        weights[3 * half + 1].wait()
        for value, q in zip(values, blocks):
            up = up + along(value, held[4 + half][rows[1], span(q)])
        hidden.append((gate / (1.0 + jnp.exp(-gate)) * up).astype(jnp.bfloat16))
    weights[2].wait()
    weights[5].wait()
    for out, places in ((send, (partner, across)), (keep, (x, far))):
        for place, q in enumerate(places):
            total = jnp.dot(hidden[0], held[4][rows[2], span(q)], preferred_element_type=jnp.float32)
            total = total + jnp.dot(hidden[1], held[5][rows[2], span(q)], preferred_element_type=jnp.float32)
            out[:, place * quarter : (place + 1) * quarter] = total.astype(jnp.bfloat16)


def expert(me, slots, pieces, weights):
    chips, _, quarter = pieces[0].shape
    count = chips * slots
    operands = [*pieces, *weights]
    out = jax.ShapeDtypeStruct((count, 2 * quarter), jnp.bfloat16)
    held = [(chips, slots, quarter)] * 4 + [weights[0].shape] * 2
    return pl.pallas_call(
        expert_kernel,
        out_shape=[out, out],
        in_specs=[SMEM] + [pl.BlockSpec(memory_space=pl.ANY)] * len(operands),
        out_specs=[VMEM, VMEM],
        scratch_shapes=[pltpu.VMEM(v, jnp.bfloat16) for v in held] + [pltpu.SemaphoreType.DMA((10,))],
        compiler_params=pltpu.CompilerParams(vmem_limit_bytes=LIMIT),
        cost_estimate=pl.CostEstimate(flops=6 * count * 2048 * 704, bytes_accessed=24_000_000, transcendentals=0),
    )(me, *operands)


def across_rows(weight, value):
    return lax.dot_general(weight, value, (((0,), (0,)), ((), ())), preferred_element_type=jnp.float32)


def mixed(weight, value):
    high = weight.astype(jnp.bfloat16)
    low = (weight - high.astype(jnp.float32)).astype(jnp.bfloat16)
    return across_rows(high, value) + across_rows(low, value)


def mix_first_kernel(x_ref, weight, value, out):
    out[...] = mixed(weight[...], value[...])


def mix_last_kernel(x_ref, total, weight, value, keep, send):
    half = keep.shape[1]
    done = total[...] + mixed(weight[...], value[...])
    keep[...] = done[:, :half]
    send[...] = done[:, half:].astype(jnp.bfloat16)


def move(value, target):
    pairs = []
    for core in range(2):
        for x in range(4):
            place = target(x, core)
            if place is not None:
                pairs.append((core * 4 + x, place[1] * 4 + place[0]))
    return lax.ppermute(value, ("c", "x"), pairs)


def partner_of(x, core):
    return (x ^ (3 if core else 1), core)


def far_of(x, core):
    return (x ^ (1 if core else 3), core)


MOVES = (
    {(2, 1): (2, 0), (3, 1): (3, 0), (1, 0): (1, 1), (2, 0): (2, 1), (1, 1): (0, 1), (3, 0): (0, 0)},
    {(3, 0): (2, 1), (2, 0): (1, 0), (1, 1): (2, 0), (0, 1): (3, 0), (0, 0): (1, 1), (2, 1): (3, 1)},
)


def shards(tokens, routes, route_weights, w_gate, w_up, w_down):
    rows, quarter = tokens.shape
    routes, route_weights = routes.T, route_weights.T
    w_gate, w_up = jnp.swapaxes(w_gate, 1, 2), jnp.swapaxes(w_up, 1, 2)
    chips = 32
    x, core = lax.axis_index("x").astype(jnp.int32), lax.axis_index("c").astype(jnp.int32)
    partner, far = x ^ (1 + 2 * core), x ^ (3 - 2 * core)
    local = (x == 0) | ((x == 1) & (core == 0)) | ((x == 3) & (core == 1))
    me = jnp.stack([x, partner, far, x ^ 2, local.astype(jnp.int32), (x == 0).astype(jnp.int32)])
    bf16, f32 = jnp.bfloat16, jnp.float32

    def shape(*dims, dtype=bf16):
        return jax.ShapeDtypeStruct(dims, dtype)

    outgoing, joined = head(routes, tokens, (w_gate[0], w_up[0], w_down[0]))
    moved, crossed = (move(joined, lambda x, core, m=m: m.get((x, core))) for m in MOVES)
    halves = [shape(chips * n, rows, dtype=f32) for n in (SLOTS, CAP - SLOTS)]
    mixing = call(weigh_kernel, halves)(me, routes, route_weights)

    def across_chips(value):
        return lax.all_to_all(value, ("y", "z"), split_axis=0, concat_axis=0, tiled=True)

    def finish(keep, received):
        return (keep.astype(f32) + received.astype(f32)).astype(bf16).reshape(chips, -1, 2 * quarter)

    tie = lax.optimization_barrier
    incoming, moved, crossed = tie((across_chips(outgoing), moved, crossed))
    weights = (joined, moved, crossed)
    halves = [shape(chips, n, quarter) for n in (SLOTS, CAP - SLOTS) for _ in range(2)]
    own, other, rest_own, rest_other = call(split_kernel, halves, moved=6_000_000)(me, incoming)
    own, far, rest_other = tie((own, move(other, far_of), rest_other))
    near, across, rest_far = move(own, partner_of), move(far, partner_of), move(rest_other, far_of)
    near, across, rest_far, rest_own = tie((near, across, rest_far, rest_own))
    keep0, send0 = expert(me, SLOTS, [own, near, far, across], weights)
    early = across_chips(finish(keep0, move(send0, partner_of)))
    rest = [rest_own, move(rest_own, partner_of), rest_far, move(rest_far, partner_of)]
    keep1, send1 = expert(me, CAP - SLOTS, rest, weights)
    late = finish(keep1, move(send1, partner_of))
    late, early = tie((late, early))
    late = across_chips(late)
    early, late = early.reshape(-1, 2 * quarter), late.reshape(-1, 2 * quarter)
    total = call(mix_first_kernel, shape(rows, 2 * quarter, dtype=f32))(me, mixing[0], early)
    keep, send = call(mix_last_kernel, [shape(rows, quarter, dtype=f32), shape(rows, quarter)])(
        me, total, mixing[1], late
    )
    return (keep + move(send, far_of).astype(f32)).astype(bf16)


def solution(mesh):
    fine = Mesh(mesh.devices.reshape(4, 8, 2, 4), ("y", "z", "c", "x"))
    expert = ("y", "z", "c")
    placed = (
        P(expert, "x"),
        P(expert, None),
        P(expert, None),
        P(expert, None, "x"),
        P(expert, None, "x"),
        P(expert, "x", None),
    )
    return jax.shard_map(shards, mesh=fine, in_specs=placed, out_specs=P(expert, "x"), check_vma=False)
```

time: 198 us -> 179 us (0.904)
  blocking collectives: 40.2 us -> 0 us
  waiting for transfers between devices: 81.6 us -> 109 us
  starting transfers between devices: 43.7 us -> 38.9 us
    all_to_all x4 -> x3, waiting for transfers between devices: 22.2 us -> 76 us  [across_chips(): lax.all_to_all(value, ('y', 'z'), split_axis=0, concat_axis=0, tiled=True)]
    all_to_all x1 -> x0, blocking collectives: 40.2 us -> none  [across_chips(): lax.all_to_all(value, ('y', 'z'), split_axis=0, concat_axis=0, tiled=True)]
    ppermute x12 -> x11, waiting for transfers between devices: 59.4 us -> 32.9 us  [move(): return lax.ppermute(value, ('c', 'x'), pairs)]
    ppermute x12 -> x11, starting transfers between devices: 16.6 us -> 13.8 us  [move(): return lax.ppermute(value, ('c', 'x'), pairs)]
    pallas_call x6 -> x4, Pallas kernels: 1.33 us -> 3.63 us  [run(): pl.pallas_call(kernel, out_shape=outs, in_specs=[SMEM] + [VMEM] * (len(ar...]
    reshape x3 -> x1, other arithmetic: 3.01 us -> 0.98 us  [finish(): (keep.astype(f32) + received.astype(f32)).astype(bf16)]
    all_to_all x4 -> x3, starting transfers between devices: 27.1 us -> 25.1 us  [across_chips(): lax.all_to_all(value, ('y', 'z'), split_axis=0, concat_axis=0, tiled=True)]
    pallas_call x3 -> x2, Pallas kernels: 20.4 us -> 18.6 us  [expert(): pl.pallas_call(expert_kernel, out_shape=[out, out], in_specs=[SMEM] + [pl...]
  transfers between devices with their start and end apart: 16 -> 14, of which waited for: 12 -> 10; matrix products, arithmetic and copies ran while one was open for 1% -> 1% of each run, Pallas kernels for 7% -> 12%
where the time goes in v3:
time: 179 us; the launch traced here: 178 us
  waiting for transfers between devices  109 us (61%)
  starting transfers between devices  38.9 us (22%)
  Pallas kernels  26.9 us (15%)
  other arithmetic  3.06 us (2%)
    all_to_all x3, waiting for transfers between devices, across_chips(): lax.all_to_all(value, ('y', 'z'), split_axis=0, concat_axis=0, tiled=True)  76 us
    ppermute x11, waiting for transfers between devices, move(): return lax.ppermute(value, ('c', 'x'), pairs)  32.9 us
    all_to_all x3, starting transfers between devices, across_chips(): lax.all_to_all(value, ('y', 'z'), split_axis=0, concat_axis=0, tiled=True)  25.1 us
    pallas_call x2, Pallas kernels, expert(): pl.pallas_call(expert_kernel, out_shape=[out, out], in_specs=[SMEM] + [pl...  18.6 us
    ppermute x11, starting transfers between devices, move(): return lax.ppermute(value, ('c', 'x'), pairs)  13.8 us
    pallas_call x1, Pallas kernels, head(): pl.pallas_call(head_kernel, out_shape=[jax.ShapeDtypeStruct((chips, 2, CA...  4.68 us
    pallas_call x4, Pallas kernels, run(): pl.pallas_call(kernel, out_shape=outs, in_specs=[SMEM] + [VMEM] * (len(ar...  3.63 us
  transfers between devices with their start and end apart: 14, of which 10 were waited for; matrix products, arithmetic and copies ran while one was open for 1% of the time, Pallas kernels for 12%

profile of v3, /device:TPU:32, one launch (start us, length us, event | category | flops | bytes accessed | tf_op | source)
XLA Modules:
  0.0 178.1 jit_solution(4301783210287803648)
XLA Ops:
  0.0 4.7 %shard_map.65 = (bf16[32,2,24,512]{3,2,1,0:T(8,128)(2,1)}, bf16[1056,2048]{1,0:T(8,128)(2,1)}) custom-call(s32[6,128]{1,0:T(8,128)} %bitcast.22, bf16[128,512]{1,0:T(8,128)(2,1)} %tokens_any.1, bf16[352,2048]{1,0:T(8,128)(2,1)} %bitcast.25, bf16[352,2048]{1,0:T(8,128)(2,1)} %bitcast.26, bf16[352,2048]{1,0:T(8,128)(2,1)} %bitcast.27), custom_call_target="tpu_custom_call" | custom-call | bytes 14000000 | tf_op jit(solution)/shard_map/pallas_call | solution.py:82
  4.7 1.3 collective-permute-start
  6.0 5.8 %collective-permute-start.1 = (bf16[1056,2048]{1,0:T(8,128)(2,1)}, bf16[1056,2048]{1,0:T(8,128)(2,1)}, u32[]{:S(2)}, u32[]{:S(2)}) collective-permute-start(bf16[1056,2048]{1,0:T(8,128)(2,1)} %get-tuple-element.33.refs_4_), channel_id=1, source_target_pairs={{0,5},{2,1},{3,6},{4,3},{5,2},{6,7},{8,13},{10,9},{11,14},{12,11},... | collective-permute-start | bytes 12976136 | tf_op jit(solution)/shard_map/ppermute | solution.py:221
  11.8 11.4 %all-to-all-start = ((bf16[32,2,24,512]{3,2,1,0:T(8,128)(2,1)}), bf16[32,2,24,512]{3,2,1,0:T(8,128)(2,1)S(1)}, u32[]{:S(2)}, u32[]{:S(2)}) async-start(bf16[32,2,24,512]{3,2,1,0:T(8,128)(2,1)} %get-tuple-element.32), calls=%async_computation | async-start | bytes 3145728 | tf_op jit(solution)/shard_map/all_to_all | solution.py:258
  23.3 39.6 %all-to-all-done.both = bf16[32,2,24,512]{3,2,1,0:T(8,128)(2,1)S(1)} async-done(((bf16[32,2,24,512]{3,2,1,0:T(8,128)(2,1)}), bf16[32,2,24,512]{3,2,1,0:T(8,128)(2,1)S(1)}, u32[]{:S(2)}, u32[]{:S(2)}) %all-to-all-start) | async-done | bytes 1572896 | tf_op jit(solution)/shard_map/all_to_all | solution.py:258
  62.9 0.6 shard_map.66
  63.6 0.6 collective-permute-start.2
  64.2 7.1 %collective-permute-done.2.refs_2_ = bf16[32,8,512]{2,1,0:T(8,128)(2,1)S(1)} collective-permute-done((bf16[32,8,512]{2,1,0:T(8,128)(2,1)S(1)}, bf16[32,8,512]{2,1,0:T(8,128)(2,1)S(1)}, u32[]{:S(2)}, u32[]{:S(2)}) %collective-permute-start.2) | collective-permute-done | bytes 262176 | tf_op jit(solution)/shard_map/ppermute | solution.py:221
  71.8 0.9 collective-permute-start.3
  72.6 1.2 collective-permute-start.4
  73.8 6.5 %collective-permute-done.3.refs_1_ = bf16[32,8,512]{2,1,0:T(8,128)(2,1)S(1)} collective-permute-done((bf16[32,8,512]{2,1,0:T(8,128)(2,1)S(1)}, bf16[32,8,512]{2,1,0:T(8,128)(2,1)S(1)}, u32[]{:S(2)}, u32[]{:S(2)}) %collective-permute-start.3) | collective-permute-done | bytes 262176 | tf_op jit(solution)/shard_map/ppermute | solution.py:221
  80.3 2.8 %collective-permute-done.4.refs_3_ = bf16[32,8,512]{2,1,0:T(8,128)(2,1)S(1)} collective-permute-done((bf16[32,8,512]{2,1,0:T(8,128)(2,1)S(1)}, bf16[32,8,512]{2,1,0:T(8,128)(2,1)S(1)}, u32[]{:S(2)}, u32[]{:S(2)}) %collective-permute-start.4) | collective-permute-done | bytes 262176 | tf_op jit(solution)/shard_map/ppermute | solution.py:221
  83.1 1.2 collective-permute-done.5.refs_2_
  84.3 0.5 collective-permute-start.6
  84.8 1.5 collective-permute-start.7
  86.3 7.5 %shard_map.68 = (bf16[256,1024]{1,0:T(8,128)(2,1)}, bf16[256,1024]{1,0:T(8,128)(2,1)}) custom-call(s32[6]{0:T(128)} %copy-done.1, bf16[32,8,512]{2,1,0:T(8,128)(2,1)} %copy-done, bf16[32,8,512]{2,1,0:T(8,128)(2,1)} %copy-done.9, bf16[32,8,512]{2,1,0:T(8,128)(2,1)} %copy-done.8, bf16[32,8,512]{2,1,0:T(8,128)(2,1)} %copy-done.10, ...), custom_call_target="tpu_custom_call" | custom-call | flops 2214592512 | bytes 24000000 | tf_op jit(solution)/shard_map/pallas_call | solution.py:182
  93.8 0.8 collective-permute-start.9
  94.6 4.6 %collective-permute-done.7.refs_3_ = bf16[32,16,512]{2,1,0:T(8,128)(2,1)} collective-permute-done((bf16[32,16,512]{2,1,0:T(8,128)(2,1)S(1)}, bf16[32,16,512]{2,1,0:T(8,128)(2,1)}, u32[]{:S(2)}, u32[]{:S(2)}) %collective-permute-start.7) | collective-permute-done | bytes 524320 | tf_op jit(solution)/shard_map/ppermute | solution.py:221
  99.2 11.2 %shard_map.67 = (bf16[512,1024]{1,0:T(8,128)(2,1)}, bf16[512,1024]{1,0:T(8,128)(2,1)}) custom-call(s32[6]{0:T(128)} %copy-done.1, bf16[32,16,512]{2,1,0:T(8,128)(2,1)} %copy-done.5, bf16[32,16,512]{2,1,0:T(8,128)(2,1)} %copy-done.12, bf16[32,16,512]{2,1,0:T(8,128)(2,1)} %copy-done.11, bf16[32,16,512]{2,1,0:T(8,128)(2,1)} %collective-permute-done.7.refs_3_, ...), custom_call_target="tpu_custom_call" | custom-call | flops 4429185024 | bytes 24000000 | tf_op jit(solution)/shard_map/pallas_call | solution.py:182
  110.4 0.6 collective-permute-start.8
  111.0 1.0 fusion
  112.0 8.9 %all-to-all-start.1 = ((bf16[32,8,1024]{2,1,0:T(8,128)(2,1)}), bf16[32,8,1024]{2,1,0:T(8,128)(2,1)S(1)}, u32[]{:S(2)}, u32[]{:S(2)}) async-start(bf16[32,8,1024]{2,1,0:T(8,128)(2,1)} %fusion), calls=%async_computation.1 | async-start | bytes 1048576 | tf_op jit(solution)/shard_map/all_to_all | solution.py:258
  120.9 4.6 %collective-permute-done.8 = bf16[512,1024]{1,0:T(8,128)(2,1)S(1)} collective-permute-done((bf16[512,1024]{1,0:T(8,128)(2,1)}, bf16[512,1024]{1,0:T(8,128)(2,1)S(1)}, u32[]{:S(2)}, u32[]{:S(2)}) %collective-permute-start.8) | collective-permute-done | bytes 1048608 | tf_op jit(solution)/shard_map/ppermute | solution.py:221
  125.5 1.4 add_convert_fusion
  126.9 10.8 %all-to-all-done.1 = bf16[32,8,1024]{2,1,0:T(8,128)(2,1)S(1)} async-done(((bf16[32,8,1024]{2,1,0:T(8,128)(2,1)}), bf16[32,8,1024]{2,1,0:T(8,128)(2,1)S(1)}, u32[]{:S(2)}, u32[]{:S(2)}) %all-to-all-start.1) | async-done | bytes 524320 | tf_op jit(solution)/shard_map/all_to_all | solution.py:258
  137.7 4.9 %all-to-all-start.2 = ((bf16[32,16,1024]{2,1,0:T(8,128)(2,1)}), bf16[32,16,1024]{2,1,0:T(8,128)(2,1)S(1)}, u32[]{:S(2)}, u32[]{:S(2)}) async-start(bf16[32,16,1024]{2,1,0:T(8,128)(2,1)} %bitcast.13), calls=%async_computation.2 | async-start | bytes 2097152 | tf_op jit(solution)/shard_map/all_to_all | solution.py:258
  142.6 1.1 shard_map.64
  143.7 0.9 shard_map.69.total
  144.6 25.6 %all-to-all-done.2 = bf16[32,16,1024]{2,1,0:T(8,128)(2,1)S(1)} async-done(((bf16[32,16,1024]{2,1,0:T(8,128)(2,1)}), bf16[32,16,1024]{2,1,0:T(8,128)(2,1)S(1)}, u32[]{:S(2)}, u32[]{:S(2)}) %all-to-all-start.2) | async-done | bytes 1048608 | tf_op jit(solution)/shard_map/all_to_all | solution.py:258
  170.2 1.0 shard_map.70
  171.3 6.2 %collective-permute-done.10 = bf16[128,512]{1,0:T(8,128)(2,1)S(1)} collective-permute-done((bf16[128,512]{1,0:T(8,128)(2,1)S(1)}, bf16[128,512]{1,0:T(8,128)(2,1)S(1)}, u32[]{:S(2)}, u32[]{:S(2)}) %collective-permute-start.10) | collective-permute-done | bytes 131104 | tf_op jit(solution)/shard_map/ppermute | solution.py:221
  177.5 0.7 add_convert_fusion.2
  (33 shorter events, 0.7 us)
Async XLA Ops:
  4.7 58.2 %collective-permute-start = (bf16[1056,2048]{1,0:T(8,128)(2,1)}, bf16[1056,2048]{1,0:T(8,128)(2,1)}, u32[]{:S(2)}, u32[]{:S(2)}) collective-permute-start(bf16[1056,2048]{1,0:T(8,128)(2,1)} %get-tuple-element.33.refs_4_), channel_id=1, source_target_pairs={{1,5},{2,6},{3,0},{5,4},{6,2},{7,3},{9,13},{10,14},{11,8},{13,12},... | collective-permute-start | bytes 12976136 | tf_op jit(solution)/shard_map/ppermute | solution.py:221
  6.0 56.9 %collective-permute-start.1 = (bf16[1056,2048]{1,0:T(8,128)(2,1)}, bf16[1056,2048]{1,0:T(8,128)(2,1)}, u32[]{:S(2)}, u32[]{:S(2)}) collective-permute-start(bf16[1056,2048]{1,0:T(8,128)(2,1)} %get-tuple-element.33.refs_4_), channel_id=1, source_target_pairs={{0,5},{2,1},{3,6},{4,3},{5,2},{6,7},{8,13},{10,9},{11,14},{12,11},... | collective-permute-start | bytes 12976136 | tf_op jit(solution)/shard_map/ppermute | solution.py:221
  11.8 51.1 %all-to-all-start = ((bf16[32,2,24,512]{3,2,1,0:T(8,128)(2,1)}), bf16[32,2,24,512]{3,2,1,0:T(8,128)(2,1)S(1)}, u32[]{:S(2)}, u32[]{:S(2)}) async-start(bf16[32,2,24,512]{3,2,1,0:T(8,128)(2,1)} %get-tuple-element.32), calls=%async_computation | async-start | bytes 3145728 | tf_op jit(solution)/shard_map/all_to_all | solution.py:258
  23.3 63.1 %copy-start.1 = (s32[6]{0:T(128)}, s32[6]{0:T(128)S(1)}, u32[]{:S(2)}) copy-start(s32[6]{0:T(128)S(1)} %stack.35.x_ref) | copy-start | bytes 76
  63.6 22.8 %copy-start = (bf16[32,8,512]{2,1,0:T(8,128)(2,1)}, bf16[32,8,512]{2,1,0:T(8,128)(2,1)S(1)}, u32[]{:S(2)}) copy-start(bf16[32,8,512]{2,1,0:T(8,128)(2,1)S(1)} %get-tuple-element.38.refs_0_) | copy-start | bytes 786436
  63.6 30.2 %copy-start.5 = (bf16[32,16,512]{2,1,0:T(8,128)(2,1)}, bf16[32,16,512]{2,1,0:T(8,128)(2,1)S(1)}, u32[]{:S(2)}) copy-start(bf16[32,16,512]{2,1,0:T(8,128)(2,1)S(1)} %get-tuple-element.42.refs_0_) | copy-start | bytes 1572868
  63.6 7.7 %collective-permute-start.2 = (bf16[32,8,512]{2,1,0:T(8,128)(2,1)S(1)}, bf16[32,8,512]{2,1,0:T(8,128)(2,1)S(1)}, u32[]{:S(2)}, u32[]{:S(2)}) collective-permute-start(bf16[32,8,512]{2,1,0:T(8,128)(2,1)S(1)} %get-tuple-element.36), channel_id=1, source_target_pairs={{0,3},{1,2},{2,1},{3,0},{4,5},{5,4},{6,7},{7,6},{8,11},{9,10},{10,... | collective-permute-start | bytes 786440 | tf_op jit(solution)/shard_map/ppermute | solution.py:221
  71.2 15.1 %copy-start.8 = (bf16[32,8,512]{2,1,0:T(8,128)(2,1)}, bf16[32,8,512]{2,1,0:T(8,128)(2,1)S(1)}, u32[]{:S(2)}) copy-start(bf16[32,8,512]{2,1,0:T(8,128)(2,1)S(1)} %collective-permute-done.2.refs_2_) | copy-start | bytes 786436
  71.2 13.0 %collective-permute-start.5 = (bf16[32,16,512]{2,1,0:T(8,128)(2,1)S(1)}, bf16[32,16,512]{2,1,0:T(8,128)(2,1)S(1)}, u32[]{:S(2)}, u32[]{:S(2)}) collective-permute-start(bf16[32,16,512]{2,1,0:T(8,128)(2,1)S(1)} %get-tuple-element.40), channel_id=1, source_target_pairs={{0,3},{1,2},{2,1},{3,0},{4,5},{5,4},{6,7},{7,6},{8,11},{9,10},{10,... | collective-permute-start | bytes 1572872 | tf_op jit(solution)/shard_map/ppermute | solution.py:221
  71.8 8.5 %collective-permute-start.3 = (bf16[32,8,512]{2,1,0:T(8,128)(2,1)S(1)}, bf16[32,8,512]{2,1,0:T(8,128)(2,1)S(1)}, u32[]{:S(2)}, u32[]{:S(2)}) collective-permute-start(bf16[32,8,512]{2,1,0:T(8,128)(2,1)S(1)} %get-tuple-element.38.refs_0_), channel_id=1, source_target_pairs={{0,1},{1,0},{2,3},{3,2},{4,7},{5,6},{6,5},{7,4},{8,9},{9,8},{10,11... | collective-permute-start | bytes 786440 | tf_op jit(solution)/shard_map/ppermute | solution.py:221
  72.6 10.4 %collective-permute-start.4 = (bf16[32,8,512]{2,1,0:T(8,128)(2,1)S(1)}, bf16[32,8,512]{2,1,0:T(8,128)(2,1)S(1)}, u32[]{:S(2)}, u32[]{:S(2)}) collective-permute-start(bf16[32,8,512]{2,1,0:T(8,128)(2,1)S(1)} %collective-permute-done.2.refs_2_), channel_id=1, source_target_pairs={{0,1},{1,0},{2,3},{3,2},{4,7},{5,6},{6,5},{7,4},{8,9},{9,8},{10,11... | collective-permute-start | bytes 786440 | tf_op jit(solution)/shard_map/ppermute | solution.py:221
  80.3 6.1 %copy-start.9 = (bf16[32,8,512]{2,1,0:T(8,128)(2,1)}, bf16[32,8,512]{2,1,0:T(8,128)(2,1)S(1)}, u32[]{:S(2)}) copy-start(bf16[32,8,512]{2,1,0:T(8,128)(2,1)S(1)} %collective-permute-done.3.refs_1_) | copy-start | bytes 786436
  83.1 3.3 %copy-start.10 = (bf16[32,8,512]{2,1,0:T(8,128)(2,1)}, bf16[32,8,512]{2,1,0:T(8,128)(2,1)S(1)}, u32[]{:S(2)}) copy-start(bf16[32,8,512]{2,1,0:T(8,128)(2,1)S(1)} %collective-permute-done.4.refs_3_) | copy-start | bytes 786436
  84.3 9.5 %copy-start.11 = (bf16[32,16,512]{2,1,0:T(8,128)(2,1)}, bf16[32,16,512]{2,1,0:T(8,128)(2,1)S(1)}, u32[]{:S(2)}) copy-start(bf16[32,16,512]{2,1,0:T(8,128)(2,1)S(1)} %collective-permute-done.5.refs_2_) | copy-start | bytes 1572868
  84.3 10.3 %collective-permute-start.6 = (bf16[32,16,512]{2,1,0:T(8,128)(2,1)S(1)}, bf16[32,16,512]{2,1,0:T(8,128)(2,1)S(1)}, u32[]{:S(2)}, u32[]{:S(2)}) collective-permute-start(bf16[32,16,512]{2,1,0:T(8,128)(2,1)S(1)} %get-tuple-element.42.refs_0_), channel_id=1, source_target_pairs={{0,1},{1,0},{2,3},{3,2},{4,7},{5,6},{6,5},{7,4},{8,9},{9,8},{10,11... | collective-permute-start | bytes 1572872 | tf_op jit(solution)/shard_map/ppermute | solution.py:221
  84.8 14.4 %collective-permute-start.7 = (bf16[32,16,512]{2,1,0:T(8,128)(2,1)S(1)}, bf16[32,16,512]{2,1,0:T(8,128)(2,1)}, u32[]{:S(2)}, u32[]{:S(2)}) collective-permute-start(bf16[32,16,512]{2,1,0:T(8,128)(2,1)S(1)} %collective-permute-done.5.refs_2_), channel_id=1, source_target_pairs={{0,1},{1,0},{2,3},{3,2},{4,7},{5,6},{6,5},{7,4},{8,9},{9,8},{10,11... | collective-permute-start | bytes 1572872 | tf_op jit(solution)/shard_map/ppermute | solution.py:221
  93.8 17.2 %copy-start.7 = (bf16[256,1024]{1,0:T(8,128)(2,1)S(1)}, bf16[256,1024]{1,0:T(8,128)(2,1)}, u32[]{:S(2)}) copy-start(bf16[256,1024]{1,0:T(8,128)(2,1)} %get-tuple-element.50) | copy-start | bytes 1572868
  93.8 17.2 %collective-permute-start.9 = (bf16[256,1024]{1,0:T(8,128)(2,1)}, bf16[256,1024]{1,0:T(8,128)(2,1)S(1)}, u32[]{:S(2)}, u32[]{:S(2)}) collective-permute-start(bf16[256,1024]{1,0:T(8,128)(2,1)} %get-tuple-element.51), channel_id=1, source_target_pairs={{0,1},{1,0},{2,3},{3,2},{4,7},{5,6},{6,5},{7,4},{8,9},{9,8},{10,11... | collective-permute-start | bytes 1572872 | tf_op jit(solution)/shard_map/ppermute | solution.py:221
  94.6 4.6 %copy-start.12 = (bf16[32,16,512]{2,1,0:T(8,128)(2,1)}, bf16[32,16,512]{2,1,0:T(8,128)(2,1)S(1)}, u32[]{:S(2)}) copy-start(bf16[32,16,512]{2,1,0:T(8,128)(2,1)S(1)} %collective-permute-done.6.refs_1_) | copy-start | bytes 1572868
  110.4 15.1 %copy-start.6 = (bf16[512,1024]{1,0:T(8,128)(2,1)S(1)}, bf16[512,1024]{1,0:T(8,128)(2,1)}, u32[]{:S(2)}) copy-start(bf16[512,1024]{1,0:T(8,128)(2,1)} %get-tuple-element.46) | copy-start | bytes 3145732
  110.4 15.1 %collective-permute-start.8 = (bf16[512,1024]{1,0:T(8,128)(2,1)}, bf16[512,1024]{1,0:T(8,128)(2,1)S(1)}, u32[]{:S(2)}, u32[]{:S(2)}) collective-permute-start(bf16[512,1024]{1,0:T(8,128)(2,1)} %get-tuple-element.47), channel_id=1, source_target_pairs={{0,1},{1,0},{2,3},{3,2},{4,7},{5,6},{6,5},{7,4},{8,9},{9,8},{10,11... | collective-permute-start | bytes 3145736 | tf_op jit(solution)/shard_map/ppermute | solution.py:221
  112.0 25.7 %all-to-all-start.1 = ((bf16[32,8,1024]{2,1,0:T(8,128)(2,1)}), bf16[32,8,1024]{2,1,0:T(8,128)(2,1)S(1)}, u32[]{:S(2)}, u32[]{:S(2)}) async-start(bf16[32,8,1024]{2,1,0:T(8,128)(2,1)} %fusion), calls=%async_computation.1 | async-start | bytes 1048576 | tf_op jit(solution)/shard_map/all_to_all | solution.py:258
  125.5 17.1 %copy-start.2 = (s32[6]{0:T(128)S(1)}, s32[6]{0:T(128)}, u32[]{:S(2)}) copy-start(s32[6]{0:T(128)} %copy-done.1) | copy-start | bytes 76
  125.5 17.1 %copy-start.3 = (s32[128,6]{0,1:T(8,128)S(1)}, s32[128,6]{0,1:T(8,128)}, u32[]{:S(2)}) copy-start(s32[128,6]{0,1:T(8,128)} %param.7) | copy-start | bytes 9220
  125.5 17.1 %copy-start.4 = (f32[128,6]{0,1:T(8,128)S(1)}, f32[128,6]{0,1:T(8,128)}, u32[]{:S(2)}) copy-start(f32[128,6]{0,1:T(8,128)} %param.8) | copy-start | bytes 9220
  137.7 32.5 %all-to-all-start.2 = ((bf16[32,16,1024]{2,1,0:T(8,128)(2,1)}), bf16[32,16,1024]{2,1,0:T(8,128)(2,1)S(1)}, u32[]{:S(2)}, u32[]{:S(2)}) async-start(bf16[32,16,1024]{2,1,0:T(8,128)(2,1)} %bitcast.13), calls=%async_computation.2 | async-start | bytes 2097152 | tf_op jit(solution)/shard_map/all_to_all | solution.py:258
  171.2 6.3 %collective-permute-start.10 = (bf16[128,512]{1,0:T(8,128)(2,1)S(1)}, bf16[128,512]{1,0:T(8,128)(2,1)S(1)}, u32[]{:S(2)}, u32[]{:S(2)}) collective-permute-start(bf16[128,512]{1,0:T(8,128)(2,1)S(1)} %get-tuple-element.56), channel_id=1, source_target_pairs={{0,3},{1,2},{2,1},{3,0},{4,5},{5,4},{6,7},{7,6},{8,11},{9,10},{10,... | collective-permute-start | bytes 393224 | tf_op jit(solution)/shard_map/ppermute | solution.py:221

commit v4 on v3

--- a/solution.py
+++ b/solution.py
@@ -185,7 +185,7 @@
         in_specs=[SMEM] + [pl.BlockSpec(memory_space=pl.ANY)] * len(operands),
         out_specs=[VMEM, VMEM],
         scratch_shapes=[pltpu.VMEM(v, jnp.bfloat16) for v in held] + [pltpu.SemaphoreType.DMA((10,))],
-        compiler_params=pltpu.CompilerParams(vmem_limit_bytes=LIMIT),
+        compiler_params=pltpu.CompilerParams(vmem_limit_bytes=24 * 1024 * 1024),
         cost_estimate=pl.CostEstimate(flops=6 * count * 2048 * 704, bytes_accessed=24_000_000, transcendentals=0),
     )(me, *operands)
 
@@ -230,8 +230,9 @@
 
 
 MOVES = (
-    {(2, 1): (2, 0), (3, 1): (3, 0), (1, 0): (1, 1), (2, 0): (2, 1), (1, 1): (0, 1), (3, 0): (0, 0)},
-    {(3, 0): (2, 1), (2, 0): (1, 0), (1, 1): (2, 0), (0, 1): (3, 0), (0, 0): (1, 1), (2, 1): (3, 1)},
+    {(2, 1): (2, 0), (0, 1): (3, 0), (0, 0): (1, 1), (2, 0): (2, 1), (1, 1): (0, 1), (3, 0): (0, 0)},
+    {(3, 0): (2, 1), (2, 0): (1, 0), (1, 1): (2, 0), (3, 1): (3, 0), (1, 0): (1, 1), (2, 1): (3, 1),
+     (0, 0): (0, 1), (0, 1): (0, 0)},
 )
 
 

time: 179 us -> 174 us (0.972)
  Pallas kernels: 26.9 us -> 23.4 us
  waiting for transfers between devices: 109 us -> 106 us
  local copies, waits for them, and re-layouts: 0.13 us -> 2.32 us
  starting transfers between devices: 38.9 us -> 36.9 us
    pallas_call x2, Pallas kernels: 18.6 us -> 15.1 us  [expert(): pl.pallas_call(expert_kernel, out_shape=[out, out], in_specs=[SMEM] + [pl...]
    ppermute x11, starting transfers between devices: 13.8 us -> 11.2 us  [move(): return lax.ppermute(value, ('c', 'x'), pairs)]
    unnamed x26 -> x6, local copies, waits for them, and re-layouts: 0.05 us -> 2.23 us
  transfers between devices with their start and end apart: 14 -> 14, of which waited for: 10 -> 10; matrix products, arithmetic and copies ran while one was open for 1% -> 2% of each run, Pallas kernels for 12% -> 10%
where the time goes in v4:
time: 174 us; the launch traced here: 173 us
  waiting for transfers between devices  106 us (61%)
  starting transfers between devices  36.9 us (21%)
  Pallas kernels  23.4 us (13%)
  other arithmetic  4.29 us (2%)
  local copies, waits for them, and re-layouts  2.32 us (1%)
    all_to_all x3, waiting for transfers between devices, across_chips(): lax.all_to_all(value, ('y', 'z'), split_axis=0, concat_axis=0, tiled=True)  74.8 us
    ppermute x11, waiting for transfers between devices, move(): return lax.ppermute(value, ('c', 'x'), pairs)  31.3 us
    all_to_all x3, starting transfers between devices, across_chips(): lax.all_to_all(value, ('y', 'z'), split_axis=0, concat_axis=0, tiled=True)  25.7 us
    pallas_call x2, Pallas kernels, expert(): pl.pallas_call(expert_kernel, out_shape=[out, out], in_specs=[SMEM] + [pl...  15.1 us
    ppermute x11, starting transfers between devices, move(): return lax.ppermute(value, ('c', 'x'), pairs)  11.2 us
    pallas_call x1, Pallas kernels, head(): pl.pallas_call(head_kernel, out_shape=[jax.ShapeDtypeStruct((chips, 2, CA...  4.67 us
    pallas_call x4, Pallas kernels, run(): pl.pallas_call(kernel, out_shape=outs, in_specs=[SMEM] + [VMEM] * (len(ar...  3.62 us
  transfers between devices with their start and end apart: 14, of which 10 were waited for; matrix products, arithmetic and copies ran while one was open for 2% of the time, Pallas kernels for 10%

profile of v4, /device:TPU:32, one launch (start us, length us, event | category | flops | bytes accessed | tf_op | source)
XLA Modules:
  0.0 173.1 jit_solution(1556541329555770413)
XLA Ops:
  0.0 4.7 %shard_map.65 = (bf16[32,2,24,512]{3,2,1,0:T(8,128)(2,1)}, bf16[1056,2048]{1,0:T(8,128)(2,1)}) custom-call(s32[6,128]{1,0:T(8,128)} %bitcast.22, bf16[128,512]{1,0:T(8,128)(2,1)} %tokens_any.1, bf16[352,2048]{1,0:T(8,128)(2,1)} %bitcast.25, bf16[352,2048]{1,0:T(8,128)(2,1)} %bitcast.26, bf16[352,2048]{1,0:T(8,128)(2,1)} %bitcast.27), custom_call_target="tpu_custom_call" | custom-call | bytes 14000000 | tf_op jit(solution)/shard_map/pallas_call | solution.py:82
  4.7 2.8 %collective-permute-start = (bf16[1056,2048]{1,0:T(8,128)(2,1)}, bf16[1056,2048]{1,0:T(8,128)(2,1)}, u32[]{:S(2)}, u32[]{:S(2)}) collective-permute-start(bf16[1056,2048]{1,0:T(8,128)(2,1)} %get-tuple-element.33.refs_4_), channel_id=1, source_target_pairs={{0,5},{2,6},{3,0},{4,3},{5,4},{6,2},{8,13},{10,14},{11,8},{12,11},... | collective-permute-start | bytes 12976136 | tf_op jit(solution)/shard_map/ppermute | solution.py:221
  7.5 2.0 %collective-permute-start.1 = (bf16[1056,2048]{1,0:T(8,128)(2,1)}, bf16[1056,2048]{1,0:T(8,128)(2,1)}, u32[]{:S(2)}, u32[]{:S(2)}) collective-permute-start(bf16[1056,2048]{1,0:T(8,128)(2,1)} %get-tuple-element.33.refs_4_), channel_id=1, source_target_pairs={{0,4},{1,5},{2,1},{3,6},{4,0},{5,2},{6,7},{7,3},{8,12},{9,13},{10,... | collective-permute-start | bytes 12976136 | tf_op jit(solution)/shard_map/ppermute | solution.py:221
  9.5 11.4 %all-to-all-start = ((bf16[32,2,24,512]{3,2,1,0:T(8,128)(2,1)}), bf16[32,2,24,512]{3,2,1,0:T(8,128)(2,1)S(1)}, u32[]{:S(2)}, u32[]{:S(2)}) async-start(bf16[32,2,24,512]{3,2,1,0:T(8,128)(2,1)} %get-tuple-element.32), calls=%async_computation | async-start | bytes 3145728 | tf_op jit(solution)/shard_map/all_to_all | solution.py:259
  21.0 38.9 %all-to-all-done.both = bf16[32,2,24,512]{3,2,1,0:T(8,128)(2,1)S(1)} async-done(((bf16[32,2,24,512]{3,2,1,0:T(8,128)(2,1)}), bf16[32,2,24,512]{3,2,1,0:T(8,128)(2,1)S(1)}, u32[]{:S(2)}, u32[]{:S(2)}) %all-to-all-start) | async-done | bytes 1572896 | tf_op jit(solution)/shard_map/all_to_all | solution.py:259
  59.9 0.6 shard_map.66
  60.5 0.9 collective-permute-start.2
  61.4 6.8 %collective-permute-done.2.refs_2_ = bf16[32,8,512]{2,1,0:T(8,128)(2,1)S(1)} collective-permute-done((bf16[32,8,512]{2,1,0:T(8,128)(2,1)S(1)}, bf16[32,8,512]{2,1,0:T(8,128)(2,1)S(1)}, u32[]{:S(2)}, u32[]{:S(2)}) %collective-permute-start.2) | collective-permute-done | bytes 262176 | tf_op jit(solution)/shard_map/ppermute | solution.py:221
  68.2 0.8 collective-permute-start.5
  69.0 2.0 %collective-permute-start.4 = (bf16[32,8,512]{2,1,0:T(8,128)(2,1)S(1)}, bf16[32,8,512]{2,1,0:T(8,128)(2,1)S(1)}, u32[]{:S(2)}, u32[]{:S(2)}) collective-permute-start(bf16[32,8,512]{2,1,0:T(8,128)(2,1)S(1)} %collective-permute-done.2.refs_2_), channel_id=1, source_target_pairs={{0,1},{1,0},{2,3},{3,2},{4,7},{5,6},{6,5},{7,4},{8,9},{9,8},{10,11... | collective-permute-start | bytes 786440 | tf_op jit(solution)/shard_map/ppermute | solution.py:221
  71.1 5.2 %collective-permute-done.3.refs_1_ = bf16[32,8,512]{2,1,0:T(8,128)(2,1)S(1)} collective-permute-done((bf16[32,8,512]{2,1,0:T(8,128)(2,1)S(1)}, bf16[32,8,512]{2,1,0:T(8,128)(2,1)S(1)}, u32[]{:S(2)}, u32[]{:S(2)}) %collective-permute-start.3) | collective-permute-done | bytes 262176 | tf_op jit(solution)/shard_map/ppermute | solution.py:221
  76.2 2.8 %collective-permute-done.4.refs_3_ = bf16[32,8,512]{2,1,0:T(8,128)(2,1)S(1)} collective-permute-done((bf16[32,8,512]{2,1,0:T(8,128)(2,1)S(1)}, bf16[32,8,512]{2,1,0:T(8,128)(2,1)S(1)}, u32[]{:S(2)}, u32[]{:S(2)}) %collective-permute-start.4) | collective-permute-done | bytes 262176 | tf_op jit(solution)/shard_map/ppermute | solution.py:221
  79.0 1.6 collective-permute-done.5.refs_2_
  80.8 1.9 %collective-permute-start.7 = (bf16[32,16,512]{2,1,0:T(8,128)(2,1)S(1)}, bf16[32,16,512]{2,1,0:T(8,128)(2,1)S(1)}, u32[]{:S(2)}, u32[]{:S(2)}) collective-permute-start(bf16[32,16,512]{2,1,0:T(8,128)(2,1)S(1)} %collective-permute-done.5.refs_2_), channel_id=1, source_target_pairs={{0,1},{1,0},{2,3},{3,2},{4,7},{5,6},{6,5},{7,4},{8,9},{9,8},{10,11... | collective-permute-start | bytes 1572872 | tf_op jit(solution)/shard_map/ppermute | solution.py:221
  82.6 2.2 %copy-done = bf16[1056,2048]{1,0:T(8,128)(2,1)S(1)} copy-done((bf16[1056,2048]{1,0:T(8,128)(2,1)S(1)}, bf16[1056,2048]{1,0:T(8,128)(2,1)}, u32[]{:S(2)}) %copy-start) | copy-done | bytes 4325400
  84.9 5.8 %shard_map.68 = (bf16[256,1024]{1,0:T(8,128)(2,1)S(1)}, bf16[256,1024]{1,0:T(8,128)(2,1)S(1)}) custom-call(s32[6]{0:T(128)S(1)} %stack.35.x_ref, bf16[32,8,512]{2,1,0:T(8,128)(2,1)S(1)} %get-tuple-element.38.refs_0_, bf16[32,8,512]{2,1,0:T(8,128)(2,1)S(1)} %collective-permute-done.3.refs_1_, bf16[32,8,512]{2,1,0:T(8,128)(2,1)S(1)} %collective-permute-done.2.refs_2_, ...), custom_call_target="tpu_custom_call" | custom-call | flops 2214592512 | bytes 24000000 | tf_op jit(solution)/shard_map/pallas_call | solution.py:182
  90.6 0.3 collective-permute-start.9
  90.9 4.5 %collective-permute-done.7.refs_3_ = bf16[32,16,512]{2,1,0:T(8,128)(2,1)S(1)} collective-permute-done((bf16[32,16,512]{2,1,0:T(8,128)(2,1)S(1)}, bf16[32,16,512]{2,1,0:T(8,128)(2,1)S(1)}, u32[]{:S(2)}, u32[]{:S(2)}) %collective-permute-start.7) | collective-permute-done | bytes 524320 | tf_op jit(solution)/shard_map/ppermute | solution.py:221
  95.4 9.3 %shard_map.67 = (bf16[512,1024]{1,0:T(8,128)(2,1)S(1)}, bf16[512,1024]{1,0:T(8,128)(2,1)S(1)}) custom-call(s32[6]{0:T(128)S(1)} %stack.35.x_ref, bf16[32,16,512]{2,1,0:T(8,128)(2,1)S(1)} %get-tuple-element.42.refs_0_, bf16[32,16,512]{2,1,0:T(8,128)(2,1)S(1)} %collective-permute-done.6.refs_1_, bf16[32,16,512]{2,1,0:T(8,128)(2,1)S(1)} %collective-permute-done.5.refs_2_, ...), custom_call_target="tpu_custom_call" | custom-call | flops 4429185024 | bytes 24000000 | tf_op jit(solution)/shard_map/pallas_call | solution.py:182
  104.7 0.3 collective-permute-start.8
  105.0 1.0 fusion
  106.0 9.4 %all-to-all-start.1 = ((bf16[32,8,1024]{2,1,0:T(8,128)(2,1)}), bf16[32,8,1024]{2,1,0:T(8,128)(2,1)S(1)}, u32[]{:S(2)}, u32[]{:S(2)}) async-start(bf16[32,8,1024]{2,1,0:T(8,128)(2,1)} %fusion), calls=%async_computation.1 | async-start | bytes 1048576 | tf_op jit(solution)/shard_map/all_to_all | solution.py:259
  115.5 4.3 %collective-permute-done.8 = bf16[512,1024]{1,0:T(8,128)(2,1)} collective-permute-done((bf16[512,1024]{1,0:T(8,128)(2,1)S(1)}, bf16[512,1024]{1,0:T(8,128)(2,1)}, u32[]{:S(2)}, u32[]{:S(2)}) %collective-permute-start.8) | collective-permute-done | bytes 1048608 | tf_op jit(solution)/shard_map/ppermute | solution.py:221
  119.7 2.6 %add_convert_fusion = bf16[512,1024]{1,0:T(8,128)(2,1)} fusion(bf16[512,1024]{1,0:T(8,128)(2,1)} %collective-permute-done.8, bf16[512,1024]{1,0:T(8,128)(2,1)S(1)} %get-tuple-element.46), kind=kLoop, calls=%fused_computation | loop fusion | flops 2097152 | bytes 3145728 | tf_op jit(solution)/shard_map/convert_element_type | solution.py:262
  122.4 10.2 %all-to-all-done.1 = bf16[32,8,1024]{2,1,0:T(8,128)(2,1)S(1)} async-done(((bf16[32,8,1024]{2,1,0:T(8,128)(2,1)}), bf16[32,8,1024]{2,1,0:T(8,128)(2,1)S(1)}, u32[]{:S(2)}, u32[]{:S(2)}) %all-to-all-start.1) | async-done | bytes 524320 | tf_op jit(solution)/shard_map/all_to_all | solution.py:259
  132.6 4.8 %all-to-all-start.2 = ((bf16[32,16,1024]{2,1,0:T(8,128)(2,1)}), bf16[32,16,1024]{2,1,0:T(8,128)(2,1)S(1)}, u32[]{:S(2)}, u32[]{:S(2)}) async-start(bf16[32,16,1024]{2,1,0:T(8,128)(2,1)} %bitcast.13), calls=%async_computation.2 | async-start | bytes 2097152 | tf_op jit(solution)/shard_map/all_to_all | solution.py:259
  137.4 1.1 shard_map.64
  138.5 0.9 shard_map.69.total
  139.4 25.8 %all-to-all-done.2 = bf16[32,16,1024]{2,1,0:T(8,128)(2,1)S(1)} async-done(((bf16[32,16,1024]{2,1,0:T(8,128)(2,1)}), bf16[32,16,1024]{2,1,0:T(8,128)(2,1)S(1)}, u32[]{:S(2)}, u32[]{:S(2)}) %all-to-all-start.2) | async-done | bytes 1048608 | tf_op jit(solution)/shard_map/all_to_all | solution.py:259
  165.2 1.0 shard_map.70
  166.3 6.2 %collective-permute-done.10 = bf16[128,512]{1,0:T(8,128)(2,1)S(1)} collective-permute-done((bf16[128,512]{1,0:T(8,128)(2,1)S(1)}, bf16[128,512]{1,0:T(8,128)(2,1)S(1)}, u32[]{:S(2)}, u32[]{:S(2)}) %collective-permute-start.10) | collective-permute-done | bytes 131104 | tf_op jit(solution)/shard_map/ppermute | solution.py:221
  172.5 0.7 add_convert_fusion.2
  (13 shorter events, 0.4 us)
Async XLA Ops:
  4.7 55.2 %collective-permute-start = (bf16[1056,2048]{1,0:T(8,128)(2,1)}, bf16[1056,2048]{1,0:T(8,128)(2,1)}, u32[]{:S(2)}, u32[]{:S(2)}) collective-permute-start(bf16[1056,2048]{1,0:T(8,128)(2,1)} %get-tuple-element.33.refs_4_), channel_id=1, source_target_pairs={{0,5},{2,6},{3,0},{4,3},{5,4},{6,2},{8,13},{10,14},{11,8},{12,11},... | collective-permute-start | bytes 12976136 | tf_op jit(solution)/shard_map/ppermute | solution.py:221
  7.5 52.4 %collective-permute-start.1 = (bf16[1056,2048]{1,0:T(8,128)(2,1)}, bf16[1056,2048]{1,0:T(8,128)(2,1)}, u32[]{:S(2)}, u32[]{:S(2)}) collective-permute-start(bf16[1056,2048]{1,0:T(8,128)(2,1)} %get-tuple-element.33.refs_4_), channel_id=1, source_target_pairs={{0,4},{1,5},{2,1},{3,6},{4,0},{5,2},{6,7},{7,3},{8,12},{9,13},{10,... | collective-permute-start | bytes 12976136 | tf_op jit(solution)/shard_map/ppermute | solution.py:221
  9.5 50.3 %all-to-all-start = ((bf16[32,2,24,512]{3,2,1,0:T(8,128)(2,1)}), bf16[32,2,24,512]{3,2,1,0:T(8,128)(2,1)S(1)}, u32[]{:S(2)}, u32[]{:S(2)}) async-start(bf16[32,2,24,512]{3,2,1,0:T(8,128)(2,1)} %get-tuple-element.32), calls=%async_computation | async-start | bytes 3145728 | tf_op jit(solution)/shard_map/all_to_all | solution.py:259
  60.5 7.7 %collective-permute-start.2 = (bf16[32,8,512]{2,1,0:T(8,128)(2,1)S(1)}, bf16[32,8,512]{2,1,0:T(8,128)(2,1)S(1)}, u32[]{:S(2)}, u32[]{:S(2)}) collective-permute-start(bf16[32,8,512]{2,1,0:T(8,128)(2,1)S(1)} %get-tuple-element.36), channel_id=1, source_target_pairs={{0,3},{1,2},{2,1},{3,0},{4,5},{5,4},{6,7},{7,6},{8,11},{9,10},{10,... | collective-permute-start | bytes 786440 | tf_op jit(solution)/shard_map/ppermute | solution.py:221
  68.2 12.4 %collective-permute-start.5 = (bf16[32,16,512]{2,1,0:T(8,128)(2,1)S(1)}, bf16[32,16,512]{2,1,0:T(8,128)(2,1)S(1)}, u32[]{:S(2)}, u32[]{:S(2)}) collective-permute-start(bf16[32,16,512]{2,1,0:T(8,128)(2,1)S(1)} %get-tuple-element.40), channel_id=1, source_target_pairs={{0,3},{1,2},{2,1},{3,0},{4,5},{5,4},{6,7},{7,6},{8,11},{9,10},{10,... | collective-permute-start | bytes 1572872 | tf_op jit(solution)/shard_map/ppermute | solution.py:221
  69.0 7.2 %collective-permute-start.3 = (bf16[32,8,512]{2,1,0:T(8,128)(2,1)S(1)}, bf16[32,8,512]{2,1,0:T(8,128)(2,1)S(1)}, u32[]{:S(2)}, u32[]{:S(2)}) collective-permute-start(bf16[32,8,512]{2,1,0:T(8,128)(2,1)S(1)} %get-tuple-element.38.refs_0_), channel_id=1, source_target_pairs={{0,1},{1,0},{2,3},{3,2},{4,7},{5,6},{6,5},{7,4},{8,9},{9,8},{10,11... | collective-permute-start | bytes 786440 | tf_op jit(solution)/shard_map/ppermute | solution.py:221
  69.0 10.0 %collective-permute-start.4 = (bf16[32,8,512]{2,1,0:T(8,128)(2,1)S(1)}, bf16[32,8,512]{2,1,0:T(8,128)(2,1)S(1)}, u32[]{:S(2)}, u32[]{:S(2)}) collective-permute-start(bf16[32,8,512]{2,1,0:T(8,128)(2,1)S(1)} %collective-permute-done.2.refs_2_), channel_id=1, source_target_pairs={{0,1},{1,0},{2,3},{3,2},{4,7},{5,6},{6,5},{7,4},{8,9},{9,8},{10,11... | collective-permute-start | bytes 786440 | tf_op jit(solution)/shard_map/ppermute | solution.py:221
  80.6 10.3 %collective-permute-start.6 = (bf16[32,16,512]{2,1,0:T(8,128)(2,1)S(1)}, bf16[32,16,512]{2,1,0:T(8,128)(2,1)S(1)}, u32[]{:S(2)}, u32[]{:S(2)}) collective-permute-start(bf16[32,16,512]{2,1,0:T(8,128)(2,1)S(1)} %get-tuple-element.42.refs_0_), channel_id=1, source_target_pairs={{0,1},{1,0},{2,3},{3,2},{4,7},{5,6},{6,5},{7,4},{8,9},{9,8},{10,11... | collective-permute-start | bytes 1572872 | tf_op jit(solution)/shard_map/ppermute | solution.py:221
  80.8 14.6 %collective-permute-start.7 = (bf16[32,16,512]{2,1,0:T(8,128)(2,1)S(1)}, bf16[32,16,512]{2,1,0:T(8,128)(2,1)S(1)}, u32[]{:S(2)}, u32[]{:S(2)}) collective-permute-start(bf16[32,16,512]{2,1,0:T(8,128)(2,1)S(1)} %collective-permute-done.5.refs_2_), channel_id=1, source_target_pairs={{0,1},{1,0},{2,3},{3,2},{4,7},{5,6},{6,5},{7,4},{8,9},{9,8},{10,11... | collective-permute-start | bytes 1572872 | tf_op jit(solution)/shard_map/ppermute | solution.py:221
  82.6 2.2 %copy-start = (bf16[1056,2048]{1,0:T(8,128)(2,1)S(1)}, bf16[1056,2048]{1,0:T(8,128)(2,1)}, u32[]{:S(2)}) copy-start(bf16[1056,2048]{1,0:T(8,128)(2,1)} %get-tuple-element.33.refs_4_) | copy-start | bytes 12976132
  90.6 14.4 %collective-permute-start.9 = (bf16[256,1024]{1,0:T(8,128)(2,1)S(1)}, bf16[256,1024]{1,0:T(8,128)(2,1)S(1)}, u32[]{:S(2)}, u32[]{:S(2)}) collective-permute-start(bf16[256,1024]{1,0:T(8,128)(2,1)S(1)} %get-tuple-element.51), channel_id=1, source_target_pairs={{0,1},{1,0},{2,3},{3,2},{4,7},{5,6},{6,5},{7,4},{8,9},{9,8},{10,11... | collective-permute-start | bytes 1572872 | tf_op jit(solution)/shard_map/ppermute | solution.py:221
  104.7 15.0 %collective-permute-start.8 = (bf16[512,1024]{1,0:T(8,128)(2,1)S(1)}, bf16[512,1024]{1,0:T(8,128)(2,1)}, u32[]{:S(2)}, u32[]{:S(2)}) collective-permute-start(bf16[512,1024]{1,0:T(8,128)(2,1)S(1)} %get-tuple-element.47), channel_id=1, source_target_pairs={{0,1},{1,0},{2,3},{3,2},{4,7},{5,6},{6,5},{7,4},{8,9},{9,8},{10,11... | collective-permute-start | bytes 3145736 | tf_op jit(solution)/shard_map/ppermute | solution.py:221
  106.0 26.6 %all-to-all-start.1 = ((bf16[32,8,1024]{2,1,0:T(8,128)(2,1)}), bf16[32,8,1024]{2,1,0:T(8,128)(2,1)S(1)}, u32[]{:S(2)}, u32[]{:S(2)}) async-start(bf16[32,8,1024]{2,1,0:T(8,128)(2,1)} %fusion), calls=%async_computation.1 | async-start | bytes 1048576 | tf_op jit(solution)/shard_map/all_to_all | solution.py:259
  119.7 17.7 %copy-start.1 = (s32[128,6]{0,1:T(8,128)S(1)}, s32[128,6]{0,1:T(8,128)}, u32[]{:S(2)}) copy-start(s32[128,6]{0,1:T(8,128)} %param.7) | copy-start | bytes 9220
  119.7 17.7 %copy-start.2 = (f32[128,6]{0,1:T(8,128)S(1)}, f32[128,6]{0,1:T(8,128)}, u32[]{:S(2)}) copy-start(f32[128,6]{0,1:T(8,128)} %param.8) | copy-start | bytes 9220
  132.6 32.6 %all-to-all-start.2 = ((bf16[32,16,1024]{2,1,0:T(8,128)(2,1)}), bf16[32,16,1024]{2,1,0:T(8,128)(2,1)S(1)}, u32[]{:S(2)}, u32[]{:S(2)}) async-start(bf16[32,16,1024]{2,1,0:T(8,128)(2,1)} %bitcast.13), calls=%async_computation.2 | async-start | bytes 2097152 | tf_op jit(solution)/shard_map/all_to_all | solution.py:259
  166.2 6.3 %collective-permute-start.10 = (bf16[128,512]{1,0:T(8,128)(2,1)S(1)}, bf16[128,512]{1,0:T(8,128)(2,1)S(1)}, u32[]{:S(2)}, u32[]{:S(2)}) collective-permute-start(bf16[128,512]{1,0:T(8,128)(2,1)S(1)} %get-tuple-element.56), channel_id=1, source_target_pairs={{0,3},{1,2},{2,1},{3,0},{4,5},{5,4},{6,7},{7,6},{8,11},{9,10},{10,... | collective-permute-start | bytes 393224 | tf_op jit(solution)/shard_map/ppermute | solution.py:221

commit v5 on v4

--- a/solution.py
+++ b/solution.py
@@ -65,13 +65,14 @@
         copy.wait()
     tokens = tokens_ref[...]
     rank, slot, _ = ranked(routes_ref, SLOTS, 1)
+    for arrived, onward in zip(into, back):
+        arrived.wait()
+        onward.start()
     chips, kinds, _, quarter = out.shape
     for step in range(3):
         pick = jnp.where(rank == (slot + step * SLOTS).astype(jnp.float32), 1.0, 0.0).astype(jnp.bfloat16)
         picked = jnp.dot(pick, tokens, preferred_element_type=jnp.float32).astype(jnp.bfloat16)
         out[:, :, step * SLOTS : (step + 1) * SLOTS, :] = picked.reshape(chips, kinds, SLOTS, quarter)
-        into[step].wait()
-        back[step].start()
     for copy in back:
         copy.wait()
 

time: 174 us -> 174 us (level)
  no operation moved by 1% of the time
where the time goes in v5:
time: 174 us; the launch traced here: 173 us
  waiting for transfers between devices  106 us (61%)
  starting transfers between devices  36.9 us (21%)
  Pallas kernels  23.4 us (13%)
  other arithmetic  4.29 us (2%)
  local copies, waits for them, and re-layouts  2.32 us (1%)
    all_to_all x3, waiting for transfers between devices, across_chips(): lax.all_to_all(value, ('y', 'z'), split_axis=0, concat_axis=0, tiled=True)  74.8 us
    ppermute x11, waiting for transfers between devices, move(): return lax.ppermute(value, ('c', 'x'), pairs)  31.3 us
    all_to_all x3, starting transfers between devices, across_chips(): lax.all_to_all(value, ('y', 'z'), split_axis=0, concat_axis=0, tiled=True)  25.7 us
    pallas_call x2, Pallas kernels, expert(): pl.pallas_call(expert_kernel, out_shape=[out, out], in_specs=[SMEM] + [pl...  15.1 us
    ppermute x11, starting transfers between devices, move(): return lax.ppermute(value, ('c', 'x'), pairs)  11.2 us
    pallas_call x1, Pallas kernels, head(): pl.pallas_call(head_kernel, out_shape=[jax.ShapeDtypeStruct((chips, 2, CA...  4.67 us
    pallas_call x4, Pallas kernels, run(): pl.pallas_call(kernel, out_shape=outs, in_specs=[SMEM] + [VMEM] * (len(ar...  3.62 us
  transfers between devices with their start and end apart: 14, of which 10 were waited for; matrix products, arithmetic and copies ran while one was open for 2% of the time, Pallas kernels for 10%

profile of v5, /device:TPU:32, one launch (start us, length us, event | category | flops | bytes accessed | tf_op | source)
XLA Modules:
  0.0 173.1 jit_solution(5064279791537309840)
XLA Ops:
  0.0 4.7 %shard_map.65 = (bf16[32,2,24,512]{3,2,1,0:T(8,128)(2,1)}, bf16[1056,2048]{1,0:T(8,128)(2,1)}) custom-call(s32[6,128]{1,0:T(8,128)} %bitcast.22, bf16[128,512]{1,0:T(8,128)(2,1)} %tokens_any.1, bf16[352,2048]{1,0:T(8,128)(2,1)} %bitcast.25, bf16[352,2048]{1,0:T(8,128)(2,1)} %bitcast.26, bf16[352,2048]{1,0:T(8,128)(2,1)} %bitcast.27), custom_call_target="tpu_custom_call" | custom-call | bytes 14000000 | tf_op jit(solution)/shard_map/pallas_call | solution.py:83
  4.7 2.8 %collective-permute-start = (bf16[1056,2048]{1,0:T(8,128)(2,1)}, bf16[1056,2048]{1,0:T(8,128)(2,1)}, u32[]{:S(2)}, u32[]{:S(2)}) collective-permute-start(bf16[1056,2048]{1,0:T(8,128)(2,1)} %get-tuple-element.33.refs_4_), channel_id=1, source_target_pairs={{0,5},{2,6},{3,0},{4,3},{5,4},{6,2},{8,13},{10,14},{11,8},{12,11},... | collective-permute-start | bytes 12976136 | tf_op jit(solution)/shard_map/ppermute | solution.py:222
  7.5 2.0 %collective-permute-start.1 = (bf16[1056,2048]{1,0:T(8,128)(2,1)}, bf16[1056,2048]{1,0:T(8,128)(2,1)}, u32[]{:S(2)}, u32[]{:S(2)}) collective-permute-start(bf16[1056,2048]{1,0:T(8,128)(2,1)} %get-tuple-element.33.refs_4_), channel_id=1, source_target_pairs={{0,4},{1,5},{2,1},{3,6},{4,0},{5,2},{6,7},{7,3},{8,12},{9,13},{10,... | collective-permute-start | bytes 12976136 | tf_op jit(solution)/shard_map/ppermute | solution.py:222
  9.5 11.4 %all-to-all-start = ((bf16[32,2,24,512]{3,2,1,0:T(8,128)(2,1)}), bf16[32,2,24,512]{3,2,1,0:T(8,128)(2,1)S(1)}, u32[]{:S(2)}, u32[]{:S(2)}) async-start(bf16[32,2,24,512]{3,2,1,0:T(8,128)(2,1)} %get-tuple-element.32), calls=%async_computation | async-start | bytes 3145728 | tf_op jit(solution)/shard_map/all_to_all | solution.py:260
  21.0 38.9 %all-to-all-done.both = bf16[32,2,24,512]{3,2,1,0:T(8,128)(2,1)S(1)} async-done(((bf16[32,2,24,512]{3,2,1,0:T(8,128)(2,1)}), bf16[32,2,24,512]{3,2,1,0:T(8,128)(2,1)S(1)}, u32[]{:S(2)}, u32[]{:S(2)}) %all-to-all-start) | async-done | bytes 1572896 | tf_op jit(solution)/shard_map/all_to_all | solution.py:260
  59.9 0.6 shard_map.66
  60.5 0.9 collective-permute-start.2
  61.4 6.8 %collective-permute-done.2.refs_2_ = bf16[32,8,512]{2,1,0:T(8,128)(2,1)S(1)} collective-permute-done((bf16[32,8,512]{2,1,0:T(8,128)(2,1)S(1)}, bf16[32,8,512]{2,1,0:T(8,128)(2,1)S(1)}, u32[]{:S(2)}, u32[]{:S(2)}) %collective-permute-start.2) | collective-permute-done | bytes 262176 | tf_op jit(solution)/shard_map/ppermute | solution.py:222
  68.2 0.8 collective-permute-start.5
  69.0 2.0 %collective-permute-start.4 = (bf16[32,8,512]{2,1,0:T(8,128)(2,1)S(1)}, bf16[32,8,512]{2,1,0:T(8,128)(2,1)S(1)}, u32[]{:S(2)}, u32[]{:S(2)}) collective-permute-start(bf16[32,8,512]{2,1,0:T(8,128)(2,1)S(1)} %collective-permute-done.2.refs_2_), channel_id=1, source_target_pairs={{0,1},{1,0},{2,3},{3,2},{4,7},{5,6},{6,5},{7,4},{8,9},{9,8},{10,11... | collective-permute-start | bytes 786440 | tf_op jit(solution)/shard_map/ppermute | solution.py:222
  71.1 5.2 %collective-permute-done.3.refs_1_ = bf16[32,8,512]{2,1,0:T(8,128)(2,1)S(1)} collective-permute-done((bf16[32,8,512]{2,1,0:T(8,128)(2,1)S(1)}, bf16[32,8,512]{2,1,0:T(8,128)(2,1)S(1)}, u32[]{:S(2)}, u32[]{:S(2)}) %collective-permute-start.3) | collective-permute-done | bytes 262176 | tf_op jit(solution)/shard_map/ppermute | solution.py:222
  76.2 2.8 %collective-permute-done.4.refs_3_ = bf16[32,8,512]{2,1,0:T(8,128)(2,1)S(1)} collective-permute-done((bf16[32,8,512]{2,1,0:T(8,128)(2,1)S(1)}, bf16[32,8,512]{2,1,0:T(8,128)(2,1)S(1)}, u32[]{:S(2)}, u32[]{:S(2)}) %collective-permute-start.4) | collective-permute-done | bytes 262176 | tf_op jit(solution)/shard_map/ppermute | solution.py:222
  79.0 1.6 collective-permute-done.5.refs_2_
  80.8 1.9 %collective-permute-start.7 = (bf16[32,16,512]{2,1,0:T(8,128)(2,1)S(1)}, bf16[32,16,512]{2,1,0:T(8,128)(2,1)S(1)}, u32[]{:S(2)}, u32[]{:S(2)}) collective-permute-start(bf16[32,16,512]{2,1,0:T(8,128)(2,1)S(1)} %collective-permute-done.5.refs_2_), channel_id=1, source_target_pairs={{0,1},{1,0},{2,3},{3,2},{4,7},{5,6},{6,5},{7,4},{8,9},{9,8},{10,11... | collective-permute-start | bytes 1572872 | tf_op jit(solution)/shard_map/ppermute | solution.py:222
  82.6 2.2 %copy-done = bf16[1056,2048]{1,0:T(8,128)(2,1)S(1)} copy-done((bf16[1056,2048]{1,0:T(8,128)(2,1)S(1)}, bf16[1056,2048]{1,0:T(8,128)(2,1)}, u32[]{:S(2)}) %copy-start) | copy-done | bytes 4325400
  84.9 5.8 %shard_map.68 = (bf16[256,1024]{1,0:T(8,128)(2,1)S(1)}, bf16[256,1024]{1,0:T(8,128)(2,1)S(1)}) custom-call(s32[6]{0:T(128)S(1)} %stack.35.x_ref, bf16[32,8,512]{2,1,0:T(8,128)(2,1)S(1)} %get-tuple-element.38.refs_0_, bf16[32,8,512]{2,1,0:T(8,128)(2,1)S(1)} %collective-permute-done.3.refs_1_, bf16[32,8,512]{2,1,0:T(8,128)(2,1)S(1)} %collective-permute-done.2.refs_2_, ...), custom_call_target="tpu_custom_call" | custom-call | flops 2214592512 | bytes 24000000 | tf_op jit(solution)/shard_map/pallas_call | solution.py:183
  90.6 0.3 collective-permute-start.9
  90.9 4.5 %collective-permute-done.7.refs_3_ = bf16[32,16,512]{2,1,0:T(8,128)(2,1)S(1)} collective-permute-done((bf16[32,16,512]{2,1,0:T(8,128)(2,1)S(1)}, bf16[32,16,512]{2,1,0:T(8,128)(2,1)S(1)}, u32[]{:S(2)}, u32[]{:S(2)}) %collective-permute-start.7) | collective-permute-done | bytes 524320 | tf_op jit(solution)/shard_map/ppermute | solution.py:222
  95.4 9.3 %shard_map.67 = (bf16[512,1024]{1,0:T(8,128)(2,1)S(1)}, bf16[512,1024]{1,0:T(8,128)(2,1)S(1)}) custom-call(s32[6]{0:T(128)S(1)} %stack.35.x_ref, bf16[32,16,512]{2,1,0:T(8,128)(2,1)S(1)} %get-tuple-element.42.refs_0_, bf16[32,16,512]{2,1,0:T(8,128)(2,1)S(1)} %collective-permute-done.6.refs_1_, bf16[32,16,512]{2,1,0:T(8,128)(2,1)S(1)} %collective-permute-done.5.refs_2_, ...), custom_call_target="tpu_custom_call" | custom-call | flops 4429185024 | bytes 24000000 | tf_op jit(solution)/shard_map/pallas_call | solution.py:183
  104.7 0.3 collective-permute-start.8
  105.0 1.0 fusion
  106.0 9.4 %all-to-all-start.1 = ((bf16[32,8,1024]{2,1,0:T(8,128)(2,1)}), bf16[32,8,1024]{2,1,0:T(8,128)(2,1)S(1)}, u32[]{:S(2)}, u32[]{:S(2)}) async-start(bf16[32,8,1024]{2,1,0:T(8,128)(2,1)} %fusion), calls=%async_computation.1 | async-start | bytes 1048576 | tf_op jit(solution)/shard_map/all_to_all | solution.py:260
  115.5 4.3 %collective-permute-done.8 = bf16[512,1024]{1,0:T(8,128)(2,1)} collective-permute-done((bf16[512,1024]{1,0:T(8,128)(2,1)S(1)}, bf16[512,1024]{1,0:T(8,128)(2,1)}, u32[]{:S(2)}, u32[]{:S(2)}) %collective-permute-start.8) | collective-permute-done | bytes 1048608 | tf_op jit(solution)/shard_map/ppermute | solution.py:222
  119.7 2.6 %add_convert_fusion = bf16[512,1024]{1,0:T(8,128)(2,1)} fusion(bf16[512,1024]{1,0:T(8,128)(2,1)} %collective-permute-done.8, bf16[512,1024]{1,0:T(8,128)(2,1)S(1)} %get-tuple-element.46), kind=kLoop, calls=%fused_computation | loop fusion | flops 2097152 | bytes 3145728 | tf_op jit(solution)/shard_map/convert_element_type | solution.py:263
  122.4 10.2 %all-to-all-done.1 = bf16[32,8,1024]{2,1,0:T(8,128)(2,1)S(1)} async-done(((bf16[32,8,1024]{2,1,0:T(8,128)(2,1)}), bf16[32,8,1024]{2,1,0:T(8,128)(2,1)S(1)}, u32[]{:S(2)}, u32[]{:S(2)}) %all-to-all-start.1) | async-done | bytes 524320 | tf_op jit(solution)/shard_map/all_to_all | solution.py:260
  132.6 4.8 %all-to-all-start.2 = ((bf16[32,16,1024]{2,1,0:T(8,128)(2,1)}), bf16[32,16,1024]{2,1,0:T(8,128)(2,1)S(1)}, u32[]{:S(2)}, u32[]{:S(2)}) async-start(bf16[32,16,1024]{2,1,0:T(8,128)(2,1)} %bitcast.13), calls=%async_computation.2 | async-start | bytes 2097152 | tf_op jit(solution)/shard_map/all_to_all | solution.py:260
  137.4 1.1 shard_map.64
  138.5 0.9 shard_map.69.total
  139.4 25.8 %all-to-all-done.2 = bf16[32,16,1024]{2,1,0:T(8,128)(2,1)S(1)} async-done(((bf16[32,16,1024]{2,1,0:T(8,128)(2,1)}), bf16[32,16,1024]{2,1,0:T(8,128)(2,1)S(1)}, u32[]{:S(2)}, u32[]{:S(2)}) %all-to-all-start.2) | async-done | bytes 1048608 | tf_op jit(solution)/shard_map/all_to_all | solution.py:260
  165.2 1.0 shard_map.70
  166.3 6.2 %collective-permute-done.10 = bf16[128,512]{1,0:T(8,128)(2,1)S(1)} collective-permute-done((bf16[128,512]{1,0:T(8,128)(2,1)S(1)}, bf16[128,512]{1,0:T(8,128)(2,1)S(1)}, u32[]{:S(2)}, u32[]{:S(2)}) %collective-permute-start.10) | collective-permute-done | bytes 131104 | tf_op jit(solution)/shard_map/ppermute | solution.py:222
  172.5 0.7 add_convert_fusion.2
  (13 shorter events, 0.4 us)
Async XLA Ops:
  4.7 55.2 %collective-permute-start = (bf16[1056,2048]{1,0:T(8,128)(2,1)}, bf16[1056,2048]{1,0:T(8,128)(2,1)}, u32[]{:S(2)}, u32[]{:S(2)}) collective-permute-start(bf16[1056,2048]{1,0:T(8,128)(2,1)} %get-tuple-element.33.refs_4_), channel_id=1, source_target_pairs={{0,5},{2,6},{3,0},{4,3},{5,4},{6,2},{8,13},{10,14},{11,8},{12,11},... | collective-permute-start | bytes 12976136 | tf_op jit(solution)/shard_map/ppermute | solution.py:222
  7.5 52.4 %collective-permute-start.1 = (bf16[1056,2048]{1,0:T(8,128)(2,1)}, bf16[1056,2048]{1,0:T(8,128)(2,1)}, u32[]{:S(2)}, u32[]{:S(2)}) collective-permute-start(bf16[1056,2048]{1,0:T(8,128)(2,1)} %get-tuple-element.33.refs_4_), channel_id=1, source_target_pairs={{0,4},{1,5},{2,1},{3,6},{4,0},{5,2},{6,7},{7,3},{8,12},{9,13},{10,... | collective-permute-start | bytes 12976136 | tf_op jit(solution)/shard_map/ppermute | solution.py:222
  9.5 50.3 %all-to-all-start = ((bf16[32,2,24,512]{3,2,1,0:T(8,128)(2,1)}), bf16[32,2,24,512]{3,2,1,0:T(8,128)(2,1)S(1)}, u32[]{:S(2)}, u32[]{:S(2)}) async-start(bf16[32,2,24,512]{3,2,1,0:T(8,128)(2,1)} %get-tuple-element.32), calls=%async_computation | async-start | bytes 3145728 | tf_op jit(solution)/shard_map/all_to_all | solution.py:260
  60.5 7.7 %collective-permute-start.2 = (bf16[32,8,512]{2,1,0:T(8,128)(2,1)S(1)}, bf16[32,8,512]{2,1,0:T(8,128)(2,1)S(1)}, u32[]{:S(2)}, u32[]{:S(2)}) collective-permute-start(bf16[32,8,512]{2,1,0:T(8,128)(2,1)S(1)} %get-tuple-element.36), channel_id=1, source_target_pairs={{0,3},{1,2},{2,1},{3,0},{4,5},{5,4},{6,7},{7,6},{8,11},{9,10},{10,... | collective-permute-start | bytes 786440 | tf_op jit(solution)/shard_map/ppermute | solution.py:222
  68.2 12.4 %collective-permute-start.5 = (bf16[32,16,512]{2,1,0:T(8,128)(2,1)S(1)}, bf16[32,16,512]{2,1,0:T(8,128)(2,1)S(1)}, u32[]{:S(2)}, u32[]{:S(2)}) collective-permute-start(bf16[32,16,512]{2,1,0:T(8,128)(2,1)S(1)} %get-tuple-element.40), channel_id=1, source_target_pairs={{0,3},{1,2},{2,1},{3,0},{4,5},{5,4},{6,7},{7,6},{8,11},{9,10},{10,... | collective-permute-start | bytes 1572872 | tf_op jit(solution)/shard_map/ppermute | solution.py:222
  69.0 7.2 %collective-permute-start.3 = (bf16[32,8,512]{2,1,0:T(8,128)(2,1)S(1)}, bf16[32,8,512]{2,1,0:T(8,128)(2,1)S(1)}, u32[]{:S(2)}, u32[]{:S(2)}) collective-permute-start(bf16[32,8,512]{2,1,0:T(8,128)(2,1)S(1)} %get-tuple-element.38.refs_0_), channel_id=1, source_target_pairs={{0,1},{1,0},{2,3},{3,2},{4,7},{5,6},{6,5},{7,4},{8,9},{9,8},{10,11... | collective-permute-start | bytes 786440 | tf_op jit(solution)/shard_map/ppermute | solution.py:222
  69.0 10.0 %collective-permute-start.4 = (bf16[32,8,512]{2,1,0:T(8,128)(2,1)S(1)}, bf16[32,8,512]{2,1,0:T(8,128)(2,1)S(1)}, u32[]{:S(2)}, u32[]{:S(2)}) collective-permute-start(bf16[32,8,512]{2,1,0:T(8,128)(2,1)S(1)} %collective-permute-done.2.refs_2_), channel_id=1, source_target_pairs={{0,1},{1,0},{2,3},{3,2},{4,7},{5,6},{6,5},{7,4},{8,9},{9,8},{10,11... | collective-permute-start | bytes 786440 | tf_op jit(solution)/shard_map/ppermute | solution.py:222
  80.6 10.3 %collective-permute-start.6 = (bf16[32,16,512]{2,1,0:T(8,128)(2,1)S(1)}, bf16[32,16,512]{2,1,0:T(8,128)(2,1)S(1)}, u32[]{:S(2)}, u32[]{:S(2)}) collective-permute-start(bf16[32,16,512]{2,1,0:T(8,128)(2,1)S(1)} %get-tuple-element.42.refs_0_), channel_id=1, source_target_pairs={{0,1},{1,0},{2,3},{3,2},{4,7},{5,6},{6,5},{7,4},{8,9},{9,8},{10,11... | collective-permute-start | bytes 1572872 | tf_op jit(solution)/shard_map/ppermute | solution.py:222
  80.8 14.6 %collective-permute-start.7 = (bf16[32,16,512]{2,1,0:T(8,128)(2,1)S(1)}, bf16[32,16,512]{2,1,0:T(8,128)(2,1)S(1)}, u32[]{:S(2)}, u32[]{:S(2)}) collective-permute-start(bf16[32,16,512]{2,1,0:T(8,128)(2,1)S(1)} %collective-permute-done.5.refs_2_), channel_id=1, source_target_pairs={{0,1},{1,0},{2,3},{3,2},{4,7},{5,6},{6,5},{7,4},{8,9},{9,8},{10,11... | collective-permute-start | bytes 1572872 | tf_op jit(solution)/shard_map/ppermute | solution.py:222
  82.6 2.2 %copy-start = (bf16[1056,2048]{1,0:T(8,128)(2,1)S(1)}, bf16[1056,2048]{1,0:T(8,128)(2,1)}, u32[]{:S(2)}) copy-start(bf16[1056,2048]{1,0:T(8,128)(2,1)} %get-tuple-element.33.refs_4_) | copy-start | bytes 12976132
  90.6 14.4 %collective-permute-start.9 = (bf16[256,1024]{1,0:T(8,128)(2,1)S(1)}, bf16[256,1024]{1,0:T(8,128)(2,1)S(1)}, u32[]{:S(2)}, u32[]{:S(2)}) collective-permute-start(bf16[256,1024]{1,0:T(8,128)(2,1)S(1)} %get-tuple-element.51), channel_id=1, source_target_pairs={{0,1},{1,0},{2,3},{3,2},{4,7},{5,6},{6,5},{7,4},{8,9},{9,8},{10,11... | collective-permute-start | bytes 1572872 | tf_op jit(solution)/shard_map/ppermute | solution.py:222
  104.7 15.0 %collective-permute-start.8 = (bf16[512,1024]{1,0:T(8,128)(2,1)S(1)}, bf16[512,1024]{1,0:T(8,128)(2,1)}, u32[]{:S(2)}, u32[]{:S(2)}) collective-permute-start(bf16[512,1024]{1,0:T(8,128)(2,1)S(1)} %get-tuple-element.47), channel_id=1, source_target_pairs={{0,1},{1,0},{2,3},{3,2},{4,7},{5,6},{6,5},{7,4},{8,9},{9,8},{10,11... | collective-permute-start | bytes 3145736 | tf_op jit(solution)/shard_map/ppermute | solution.py:222
  106.0 26.6 %all-to-all-start.1 = ((bf16[32,8,1024]{2,1,0:T(8,128)(2,1)}), bf16[32,8,1024]{2,1,0:T(8,128)(2,1)S(1)}, u32[]{:S(2)}, u32[]{:S(2)}) async-start(bf16[32,8,1024]{2,1,0:T(8,128)(2,1)} %fusion), calls=%async_computation.1 | async-start | bytes 1048576 | tf_op jit(solution)/shard_map/all_to_all | solution.py:260
  119.7 17.7 %copy-start.1 = (s32[128,6]{0,1:T(8,128)S(1)}, s32[128,6]{0,1:T(8,128)}, u32[]{:S(2)}) copy-start(s32[128,6]{0,1:T(8,128)} %param.7) | copy-start | bytes 9220
  119.7 17.7 %copy-start.2 = (f32[128,6]{0,1:T(8,128)S(1)}, f32[128,6]{0,1:T(8,128)}, u32[]{:S(2)}) copy-start(f32[128,6]{0,1:T(8,128)} %param.8) | copy-start | bytes 9220
  132.6 32.6 %all-to-all-start.2 = ((bf16[32,16,1024]{2,1,0:T(8,128)(2,1)}), bf16[32,16,1024]{2,1,0:T(8,128)(2,1)S(1)}, u32[]{:S(2)}, u32[]{:S(2)}) async-start(bf16[32,16,1024]{2,1,0:T(8,128)(2,1)} %bitcast.13), calls=%async_computation.2 | async-start | bytes 2097152 | tf_op jit(solution)/shard_map/all_to_all | solution.py:260
  166.2 6.3 %collective-permute-start.10 = (bf16[128,512]{1,0:T(8,128)(2,1)S(1)}, bf16[128,512]{1,0:T(8,128)(2,1)S(1)}, u32[]{:S(2)}, u32[]{:S(2)}) collective-permute-start(bf16[128,512]{1,0:T(8,128)(2,1)S(1)} %get-tuple-element.56), channel_id=1, source_target_pairs={{0,3},{1,2},{2,1},{3,0},{4,5},{5,4},{6,7},{7,6},{8,11},{9,10},{10,... | collective-permute-start | bytes 393224 | tf_op jit(solution)/shard_map/ppermute | solution.py:222
